TPU v7x, 128 devices: a whole 4x4x4 slice. The times are simulated.
128 devices in a mesh: dp: 16 (over z, y), seq: 8 (over x, core).
Axes of the slice: x: 4, y: 4, z: 4, core: 2. Of those that a mesh axis runs over, the one named last changes fastest.
Arguments:
- inputs: bfloat16 [16, 1024, 1024], P('dp', 'seq'), may hold values from -6 to 6
- cotangent: bfloat16 [16, 1024, 1024], P('dp', 'seq'), may hold values from -6 to 6
- ln1_gain: bfloat16 [1024], P(('dp', 'seq')), may hold values from 0.25 to 1.75
- ln1_bias: bfloat16 [1024], P(('dp', 'seq')), may hold values from -3 to 3
- w_query: bfloat16 [1024, 1024], P(('dp', 'seq')), may hold values from -0.1875 to 0.1875
- w_key: bfloat16 [1024, 1024], P(('dp', 'seq')), may hold values from -0.1875 to 0.1875
- w_value: bfloat16 [1024, 1728], P(('dp', 'seq')), may hold values from -0.1875 to 0.1875
- w_gate: bfloat16 [1024, 1728], P(('dp', 'seq')), may hold values from -0.1875 to 0.1875
- w_out: bfloat16 [1728, 1024], P(None, ('dp', 'seq')), may hold values from -0.3125 to 0.3125
- ln2_gain: bfloat16 [1024], P(('dp', 'seq')), may hold values from 0.25 to 1.75
- ln2_bias: bfloat16 [1024], P(('dp', 'seq')), may hold values from -3 to 3
- w_mlp_gate: bfloat16 [1024, 1728], P(('dp', 'seq')), may hold values from -0.1875 to 0.1875
- w_mlp_up: bfloat16 [1024, 1728], P(('dp', 'seq')), may hold values from -0.1875 to 0.1875
- w_mlp_down: bfloat16 [1728, 1024], P(None, ('dp', 'seq')), may hold values from -0.3125 to 0.3125
Outputs:
- outputs: bfloat16 [16, 1024, 1024], P('dp', 'seq')
- grad_inputs: bfloat16 [16, 1024, 1024], P('dp', 'seq')
- grad_ln1_gain: float32 [1024], P(('dp', 'seq'))
- grad_ln1_bias: float32 [1024], P(('dp', 'seq'))
- grad_w_query: float32 [1024, 1024], P(('dp', 'seq'))
- grad_w_key: float32 [1024, 1024], P(('dp', 'seq'))
- grad_w_value: float32 [1024, 1728], P(('dp', 'seq'))
- grad_w_gate: float32 [1024, 1728], P(('dp', 'seq'))
- grad_w_out: float32 [1728, 1024], P(None, ('dp', 'seq'))
- grad_ln2_gain: float32 [1024], P(('dp', 'seq'))
- grad_ln2_bias: float32 [1024], P(('dp', 'seq'))
- grad_w_mlp_gate: float32 [1024, 1728], P(('dp', 'seq'))
- grad_w_mlp_up: float32 [1024, 1728], P(('dp', 'seq'))
- grad_w_mlp_down: float32 [1728, 1024], P(None, ('dp', 'seq'))
All inputs are finite; a program needn't handle non-finite values.
Results may differ from a plain program's by a relative error of at most 0.019.
Values may be sent and summed in bfloat16 or wider, within the bound.
A program may use at most 192 MiB of HBM per device.

v0:
```python
import functools

import jax
import jax.numpy as jnp
import numpy as np
from jax import lax
from jax.experimental import pallas as pl
from jax.experimental.pallas import tpu as pltpu
from jax.sharding import PartitionSpec as P

MESH = pl.DeviceIdType.MESH
F32 = jnp.float32
BF16 = jnp.bfloat16
EPS = 1e-05
VH = 432

CK, CV, CQ, CG, CO, CMG, CMU, CMD, TOTAL = 0, 512, 1408, 1920, 2816, 3712, 4608, 5504, 6400
WIDE = 896
REAL = 864
VTILE = CV + 768
OVEC, OK, OV, OQ, OG, OO, OMG, OMU, OMD, OTOTAL = (
    0, 128, 1152, 2944, 3968, 5760, 7552, 9344, 11136, 12928,
)


def cut(start, *tiles):
    parts = []
    for part, n in enumerate(tiles):
        parts.append((part, start, 128 * n))
        start += 128 * n
    return tuple(parts)


GATHERS = (cut(CK, 4, 4, 3), cut(CQ, 4, 3, 4), cut(CO, 3, 1, 3), cut(CMG, 6, 3, 5), cut(CMD, 2, 3, 2))
KV = cut(CK, 4, 4, 3)
KV_EARLY, KV_LATE = cut(CK, 4, 4, 2), ((2, VTILE, 128),)
QG, OUT, MLP, DOWN = cut(CQ, 5, 3, 3), cut(CO, 2, 2, 3), cut(CMG, 6, 2, 6), cut(CMD, 3, 2, 2)
PIECES = ((slice(0, 224), 0), (slice(224, 432), 0), (slice(432, 656), 1), (slice(656, 864), 1))
ORDERS = (("x", "y", "z"), ("y", "z", "x"), ("z", "x", "y"))
ZYX = ("z", "y", "x")


def tables():
    half = 128
    inverse = np.power(10000.0, -np.arange(half, dtype=np.float64) / half)
    angles = np.arange(1024, dtype=np.float64)[:, None] * inverse[None, :]
    return (
        np.cos(angles).astype(np.float32).reshape(4, 256, half),
        np.sin(angles).astype(np.float32).reshape(4, 256, half),
    )


def mm(a, b):
    return lax.dot_general(a, b, (((1,), (0,)), ((), ())), preferred_element_type=F32)


def mm_nt(a, b):
    return lax.dot_general(a, b, (((1,), (1,)), ((), ())), preferred_element_type=F32)


def loop(n, body):
    def step(i, carry):
        body(i)
        return carry

    lax.fori_loop(0, n, step, 0)


def kernel(
    x_in, g_in, vec_in, wq_in, wk_in, wv_in, wg_in, wo_in, wmg_in, wmu_in, wmd_in, cos_in, sin_in,
    out_ref, gin_ref, pack_ref, *scratch,
):
    (
        W, Gd, RA, RB1, R2, R3, X, G, WS, IN8, INW, INV, PACK, OUTV, PSEND, PRECV, VEC, VA, COS, SIN, STAT,
        NORM, NORMT, TT, Q, QS, K, KW, V, GGP, GATE, WT, MASK, MIX, GRP,
        UT, TOT, STATES, CT, GUT, GATED, MID, SB, RB, SBO, RBO, OWN1, RB2, RB3, OWN2,
        SEC, ACT, BCT, HID, GGL, GUL, GM, GMX, GQ, GK, GV, FSEND, FRECV, KEEP,
        way_s, way_r, st_s, st_r, ex_s, ex_r, loc,
    ) = scratch
    S1, S2, VT, RSTD, GML = RB1.at[0], R2.at[0], TT.at[0:WIDE], MIX, SEC
    dp = lax.axis_index("dp")
    sq = lax.axis_index("seq")
    me = {"z": dp // 4, "y": dp % 4, "x": sq // 2}
    c = sq % 2
    c0 = (c == 0).astype(F32)
    c1 = (c == 1).astype(F32)

    def shifted(axis, k):
        p = dict(me)
        p[axis] = (me[axis] + k) % 4
        return p

    def device(p, core):
        return (p["z"] * 4 + p["y"], p["x"] * 2 + core)

    sibling = device(me, 1 - c)

    def remote(src, dst, ss, rs, dev):
        return pltpu.make_async_remote_copy(
            src_ref=src, dst_ref=dst, send_sem=ss, recv_sem=rs, device_id=dev, device_id_type=MESH
        )

    rows_own = pl.ds(pl.multiple_of(c * 128, 128), 128)
    rows_sib = pl.ds(pl.multiple_of((1 - c) * 128, 128), 128)
    fetch = [
        pltpu.make_async_copy(src, dst, loc.at[i])
        for i, (src, dst) in enumerate(
            (
                (wq_in, IN8.at[0]), (wk_in, IN8.at[1]), (wv_in, INW.at[0]), (wg_in, INW.at[1]),
                (wo_in, INW.at[2]), (wmg_in, INW.at[3]), (wmu_in, INW.at[4]), (wmd_in, INW.at[5]),
                (vec_in, INV), (x_in, X.at[rows_own, :]), (g_in, G.at[rows_own, :]),
                (cos_in.at[me["x"]], COS), (sin_in.at[me["x"]], SIN),
            )
        )
    ]
    for copy in fetch:
        copy.start()
    barrier = pltpu.get_barrier_semaphore()
    pl.semaphore_signal(barrier, inc=1, device_id=sibling, device_id_type=MESH)
    for axis in ZYX:
        for k in (1, 2, 3):
            pl.semaphore_signal(
                barrier, inc=1, device_id=device(shifted(axis, k), c), device_id_type=MESH
            )

    def put(ref, col, own):
        both = jnp.concatenate([own * c0, own * c1], axis=0)
        ref[:, col : col + own.shape[1]] = both.astype(BF16)

    def pack(col, h0, h1):
        put(PRECV.at[0], col, h0 * c0 + h1 * c1)
        put(PSEND, col, h0 * c1 + h1 * c0)

    for copy in fetch[:9]:
        copy.wait()
    for i, col in enumerate((CQ, CK)):
        w = IN8[i].astype(F32)
        pack(col, w[:, :512], w[:, 512:])
    lane = lax.broadcasted_iota(jnp.int32, (8, WIDE), 1)
    for i, col in enumerate((CV, CG, CO, CMG, CMU, CMD)):
        WS[:, 1664:1792] = jnp.zeros((8, 128), F32)
        WS[:, :1728] = INW[i].astype(F32)
        h0 = jnp.where(lane < REAL, WS[:, :WIDE], 0.0)
        h1 = pltpu.roll(WS[:, 768:1792], 1024 - 96, 1)[:, :WIDE]
        h1 = jnp.where(lane < REAL, h1, 0.0)
        if col == CV:
            v = jnp.concatenate([INV[...], jnp.zeros((120, 128), F32)], axis=0).T
            v = pltpu.roll(v[0:8, :], 96, 1)
            v = jnp.concatenate([jnp.zeros((8, 768), F32), v], axis=1)
            h0 = h0 + v
            h1 = h1 + v
        pack(col, h0, h1)
    pl.semaphore_wait(barrier, 10)

    e_pack = remote(PSEND, PRECV.at[1], ex_s.at[0], ex_r.at[0], sibling)
    e_x = remote(X.at[rows_own, :], X.at[rows_own, :], ex_s.at[1], ex_r.at[1], sibling)
    e_g = remote(G.at[rows_own, :], G.at[rows_own, :], ex_s.at[2], ex_r.at[2], sibling)
    e_pack.start()
    fetch[9].wait()
    e_x.start()
    fetch[10].wait()
    e_g.start()
    e_pack.wait_recv()
    for col in range(0, TOTAL, 1280):
        s = pl.ds(col, 1280)
        W[me["z"], me["y"], me["x"], :, s] = (
            PRECV[0, :, s].astype(F32) + PRECV[1, :, s].astype(F32)
        ).astype(BF16)

    pending = []
    count = [0]

    def stage(total):
        count[0] += 1
        return way_s.at[count[0] - 1], way_r.at[count[0] - 1], total

    def send(where, src, dst, dev):
        remote(src, dst, where[0], where[1], dev).start()

    def arrived(where):
        ss, rs, total = where
        remote(total, total, ss, rs, sibling).wait_recv()
        pending.append(where)

    def columns(parts):
        return pl.ds(parts[0][1], sum(n for _, _, n in parts))

    def gather(group, phase, forward=False):
        s = columns(GATHERS[group])
        if phase == 0:
            where = stage(W.at[0, 0, 0:3, :, s])
        elif phase == 1:
            where = stage(W.at[0, 0:3, :, :, s])
        else:
            where = stage(W.at[0, :, :, :, s] if forward else W.at[0:2, :, :, :, s])
        for part, col, n in GATHERS[group]:
            order = ORDERS[part]
            axis = order[phase]
            for i, k in enumerate((1, 3) if phase == 2 else (1, 2, 3)):
                idx = []
                for a in ZYX:
                    if a == axis and forward:
                        idx.append((me[a] - k) % 4)
                    elif a in order[:phase]:
                        idx.append(slice(None))
                    else:
                        idx.append(me[a])
                if forward:
                    at = 0 if axis != "z" else 1
                    idx[at] = pl.ds(2 * i, 2)
                src = W.at[tuple(idx) + (slice(None), pl.ds(col, n))]
                send(where, src, src, device(shifted(axis, k), c))
        return where

    p1 = [gather(g, 0) for g in range(5)]
    p2, p3, p4 = {}, {}, {}
    def step1(g):
        arrived(p1[g])
        p2[g] = gather(g, 1)

    def step2(g):
        arrived(p2[g])
        p3[g] = gather(g, 2)

    def step3(g):
        arrived(p3[g])
        p4[g] = gather(g, 2, True)

    step1(0)
    step1(2)
    step1(1)
    step2(0)
    step2(1)

    e_x.wait_recv()
    e_g.wait_recv()
    fetch[11].wait()
    fetch[12].wait()

    def wcols(col, n):
        return W[:, :, :, :, col : col + n].reshape(1024, n)

    def wrows(i, col, n):
        return W[i, :, :, :, col : col + n].reshape(256, n)

    def fwd(a, col, n, emit):
        for at in range(0, n, 256):
            w = min(256, n - at)
            emit(at, w, mm(a[...], wcols(col + at, w)))

    def grad(at, b, col):
        n = b.shape[1]

        def body(i):
            r = mm(at[pl.ds(pl.multiple_of(i * 256, 256), 256), :], b[...])
            Gd[i, :, :, :, col : col + n] = r.astype(BF16).reshape(4, 4, 16, n)

        loop(4, body)

    def rows(i, n=32):
        return pl.ds(pl.multiple_of(i * n, n), n)

    lanes = lax.broadcasted_iota(jnp.int32, (32, WIDE), 1)
    in0 = lanes < VH
    in1 = (lanes >= VH) & (lanes < REAL)
    real = lanes < REAL

    def log_gamma(hh):
        g0 = float(np.log(1.0 - 2.0 ** (-5.0 - hh)))
        g1 = float(np.log(1.0 - 2.0 ** (-7.0 - hh)))
        return jnp.where(c == 0, jnp.float32(g0), jnp.float32(g1))

    lg = [log_gamma(0), log_gamma(1)]

    def mask_body(i):
        ii = lax.broadcasted_iota(jnp.int32, (32, 256), 0) + i * 32
        jj = lax.broadcasted_iota(jnp.int32, (32, 256), 1)
        d = (ii - jj).astype(F32)
        for hh in range(2):
            MASK[hh, rows(i), :] = jnp.where(d >= 0, jnp.exp(jnp.maximum(d, 0.0) * lg[hh]), 0.0)

    loop(8, mask_body)
    VA[...] = jnp.zeros_like(VA)

    def norm(v):
        mean = jnp.mean(v, axis=-1, keepdims=True)
        center = v - mean
        spread = jnp.mean(center * center, axis=-1, keepdims=True)
        rstd = lax.rsqrt(spread + EPS)
        return center * rstd, rstd, mean

    def ln1_stats(i):
        xh, rstd, mean = norm(X[rows(i), :].astype(F32))
        GM[rows(i), :] = xh
        STAT[0, rows(i), :] = jnp.broadcast_to(mean, (32, 128))
        STAT[1, rows(i), :] = jnp.broadcast_to(rstd, (32, 128))

    loop(8, ln1_stats)
    step3(0)
    step1(3)
    step3(1)
    step2(2)
    arrived(p4[0])
    VEC[...] = wcols(VTILE, 128).astype(F32).T[96:104, :]
    gain1, bias1 = VEC[0:1, :], VEC[1:2, :]
    gain2, bias2 = VEC[2:3, :], VEC[3:4, :]

    def ln1(i):
        NORM[rows(i), :] = (GM[rows(i), :] * gain1 + bias1).astype(BF16)

    loop(8, ln1)

    def transpose(src, dst):
        dst[...] = src[...].T

    def rotated(dst, dst2, offset, sign, scale):
        def emit(at, w, r):
            hh = at // 256
            u, z = r[:, :128], r[:, 128:]
            co, si = COS[...], SIN[...]
            a0 = ((u * co - z * si) * scale).astype(BF16)
            a1 = ((u * si + z * co) * scale).astype(BF16)
            spot = lax.broadcasted_iota(jnp.int32, (256, 128), 0).astype(F32)
            sc = jnp.exp((spot * sign + offset) * lg[hh])
            dst[:, at : at + 128] = a0
            dst[:, at + 128 : at + 256] = a1
            dst2[:, at : at + 128] = (a0.astype(F32) * sc).astype(BF16)
            dst2[:, at + 128 : at + 256] = (a1.astype(F32) * sc).astype(BF16)

        return emit

    fwd(NORM, CK, 512, rotated(K, KW, 255.0, -1.0, 0.0625))

    def emit_v(at, w, r):
        col = lax.broadcasted_iota(jnp.int32, (256, w), 1) + at
        V[:, at : at + w] = jnp.where(col < REAL, r, 0.0).astype(BF16)

    fwd(NORM, CV, WIDE, emit_v)
    transpose(V, VT)
    for hh in range(2):
        r = mm(VT[VH * hh : VH * (hh + 1), :], KW[:, 256 * hh : 256 * (hh + 1)])
        UT[VH * hh : VH * (hh + 1), :] = r.astype(BF16)

    def states(src, base, back):
        x = me["x"]
        near = dict(me, x=x + 1 - 2 * (x % 2))
        far = dict(me, x=3 - x)
        low = x < 2
        sends = (x != 0) if back else (x != 3)
        gets = (x != 1) if back else (x != 2)
        passes = ~low if back else low
        steps = []
        for i, (at, hh) in enumerate(PIECES):
            t = base + i
            slot = 1 if back else 0
            one = remote(src.at[at], STATES.at[slot, at], st_s.at[t], st_r.at[t], device(near, c))
            pl.when(sends)(one.start)
            steps.append(one)

        def second(i):
            at, hh = PIECES[i]
            t = base + 4 + i
            two = remote(TOT.at[at], STATES.at[2, at], st_s.at[t], st_r.at[t], device(far, c))

            def total():
                steps[i].wait_recv()
                own = src[at, :].astype(F32)
                got = STATES[slot, at, :].astype(F32)
                g = jnp.exp(256.0 * lg[hh])
                first = (x % 2 == 1) if back else (x % 2 == 0)
                TOT[at, :] = jnp.where(first, own * g + got, own + got * g).astype(BF16)
                two.start()

            pl.when(passes)(total)
            return two

        def finish(dst):
            dst[...] = jnp.zeros_like(dst)
            for i, two in enumerate(twos):
                at, hh = PIECES[i]
                g = jnp.exp(256.0 * lg[hh])

                def single():
                    dst[at, :] = STATES[slot, at, :]

                def double():
                    two.wait_recv()
                    dst[at, :] = STATES[2, at, :]

                def triple():
                    steps[i].wait_recv()
                    two.wait_recv()
                    total = STATES[2, at, :].astype(F32) * g
                    dst[at, :] = (total + STATES[slot, at, :].astype(F32)).astype(BF16)

                one, pair, three = (2, 1, 0) if back else (1, 2, 3)
                pl.when(x == one)(single)
                pl.when(x == pair)(double)
                pl.when(x == three)(triple)

        def sent():
            for one, two in zip(steps, twos):
                pl.when(sends)(one.wait_send)
                pl.when(passes)(two.wait_send)

        twos = []

        def middle(*pieces):
            twos.extend(second(i) for i in pieces)

        return middle, finish, sent

    u_middle, u_finish, u_sent = states(UT, 0, False)
    step1(4)
    step2(3)
    u_middle(0, 1, 2, 3)
    step3(2)
    transpose(NORM, NORMT)
    transpose(G, TT)
    step2(4)
    arrived(p4[1])
    fwd(NORM, CQ, 512, rotated(Q, QS, 1.0, 1.0, 1.0))

    for hh in range(2):
        raw = mm_nt(Q[:, 256 * hh : 256 * (hh + 1)], K[:, 256 * hh : 256 * (hh + 1)])
        WT[hh] = (raw * MASK[hh]).astype(BF16)

    def join(dst, h0, h1):
        pick = lax.broadcasted_iota(jnp.int32, (256, 128), 1) < VH - 384
        dst[:, 0:384] = h0[:, :384]
        dst[:, 384:512] = jnp.where(pick, h0[:, 384:512], h1[:, :128])
        dst[:, 512:896] = h1[:, 128:512]

    join(MIX, mm(WT[0], V[:, 0:512]), mm(WT[1], V[:, 384:896]))

    def emit_gate(at, w, r):
        GATE[:, at : at + w] = r

    fwd(NORM, CG, WIDE, emit_gate)
    u_finish(CT)
    step3(3)
    join(GRP, mm_nt(QS[:, 0:256], CT[0:512, :]), mm_nt(QS[:, 256:512], CT[384:896, :]))

    def heads_mean(v):
        m0 = jnp.sum(jnp.where(in0, v, 0.0), axis=-1, keepdims=True) * (1.0 / VH)
        m1 = jnp.sum(jnp.where(in1, v, 0.0), axis=-1, keepdims=True) * (1.0 / VH)
        return jnp.where(in0, m0, m1)

    def group_norm(i):
        m = MIX[rows(i), :] + GRP[rows(i), :]
        center = m - heads_mean(m)
        rstd = lax.rsqrt(heads_mean(center * center) + EPS)
        grouped = jnp.where(real, center * rstd, 0.0)
        GRP[rows(i), :] = grouped
        RSTD[rows(i), :] = rstd
        gate = GATE[rows(i), :]
        GATED[rows(i), :] = (gate * jax.nn.sigmoid(gate) * grouped).astype(BF16)

    loop(8, group_norm)
    arrived(p4[2])

    def out_body(i):
        r = mm_nt(GATED[...], wrows(i, CO, WIDE))
        s = pl.ds(pl.multiple_of(i * 256, 256), 256)
        MID[:, s] = r
        SB[:, s] = r.astype(BF16)
        remote(SB.at[:, s], RB.at[:, s], ex_s.at[3], ex_r.at[3], sibling).start()

    loop(4, out_body)
    e_mid = remote(SB, RB, ex_s.at[3], ex_r.at[3], sibling)
    step3(4)
    e_mid.wait_recv()

    def ln2(i):
        m = X[rows(i), :].astype(F32) + MID[rows(i), :] + RB[rows(i), :].astype(F32)
        MID[rows(i), :] = m
        xh, rstd, mean = norm(m)
        STAT[2, rows(i), :] = jnp.broadcast_to(mean, (32, 128))
        STAT[3, rows(i), :] = jnp.broadcast_to(rstd, (32, 128))
        SEC[rows(i), :] = (xh * gain2 + bias2).astype(BF16)

    loop(8, ln2)
    arrived(p4[3])

    def emit_act(at, w, r):
        ACT[:, at : at + w] = r

    def emit_bct(at, w, r):
        BCT[:, at : at + w] = r

    fwd(SEC, CMG, WIDE, emit_act)
    fwd(SEC, CMU, WIDE, emit_bct)

    def gelu(i):
        g = ACT[rows(i), :]
        u = BCT[rows(i), :]
        cdf = 0.5 * (1.0 + lax.erf(g * 0.7071067811865476))
        ge = g * cdf
        HID[rows(i), :] = (ge * u).astype(BF16)
        BCT[rows(i), :] = ge
        ACT[rows(i), :] = (cdf + g * jnp.exp(-0.5 * g * g) * 0.3989422804014327) * u

    loop(8, gelu)
    arrived(p4[4])

    def place(axes, where):
        return tuple(where.get(a, slice(None)) for a in axes)

    def others(part, phase):
        order = ORDERS[part][::-1]
        return order[phase], [a for a in ZYX if a not in order[: phase + 1]], [a for a in ZYX if a not in order[:phase]]

    def scatter0(parts, late=None):
        s = columns(parts)
        early = stage(RA.at[:, :, :, :, s])
        late = late or stage(RB1.at[:, :, :, :, s])
        for where in (early, late):
            for part, col, n in parts:
                axis, rest, left = others(part, 0)
                s = (slice(None), pl.ds(col, n))
                for i, k in enumerate((1, 3)):
                    dev = device(shifted(axis, k), c)
                    if where is early:
                        src = Gd.at[place(left, {axis: (me[axis] + 2) % 4, rest[0]: pl.ds(2 * i, 2)}) + s]
                        send(where, src, RA.at[(i, slice(None), slice(None)) + s], dev)
                    else:
                        near = pl.ds(2 - 2 * i, 2)
                        src = Gd.at[place(left, {axis: (me[axis] + k) % 4, rest[0]: near}) + s]
                        send(where, src, RB1.at[(i, near, slice(None)) + s], dev)
        return early, late

    def scatter1(parts, where):
        early, late = where
        arrived(early)
        for part, col, n in parts:
            axis, rest, left = others(part, 0)
            s = (slice(None), pl.ds(col, n))
            for i, k in enumerate((1, 3)):

                def body(j):
                    own = Gd[place(left, {axis: (me[axis] + k) % 4, rest[0]: 2 * i + j}) + s]
                    at = (i, j, slice(None)) + s
                    RA[at] = (own.astype(F32) + RA[at].astype(F32)).astype(BF16)

                loop(2, body)
                src = RA.at[(i, slice(None), slice(None)) + s]
                dst = RB1.at[(i, pl.ds(2 * i, 2), slice(None)) + s]
                send(late, src, dst, device(shifted(axis, k), c))
        return late

    def scatter2(parts, late):
        arrived(late)
        where = stage(R2.at[:, :, :, columns(parts)])
        for part, col, n in parts:
            axis, rest, left = others(part, 0)
            s = (slice(None), pl.ds(col, n))

            def body(j):
                own = Gd[place(left, {axis: me[axis], rest[0]: j}) + s].astype(F32)
                at = (j, slice(None)) + s
                RB1[(0,) + at] = (own + RB1[(0,) + at].astype(F32) + RB1[(1,) + at].astype(F32)).astype(BF16)

            loop(4, body)
            axis, rest, left = others(part, 1)
            for k in (1, 2, 3):
                to = shifted(axis, k)
                src = S1.at[place(left, {axis: to[axis]}) + s]
                send(where, src, R2.at[(k - 1, slice(None)) + s], device(to, c))
        return where

    def scatter3(parts, where):
        arrived(where)
        where = stage(R3.at[:, :, columns(parts)])
        for part, col, n in parts:
            axis, rest, left = others(part, 1)
            s = (slice(None), pl.ds(col, n))
            t = S1[place(left, {axis: me[axis]}) + s].astype(F32)
            for k in range(3):
                t = t + R2[(k, slice(None)) + s].astype(F32)
            S2[(slice(None),) + s] = t.astype(BF16)
            axis, rest, left = others(part, 2)
            for k in (1, 2, 3):
                to = shifted(axis, k)
                send(where, S2.at[(to[axis],) + s], R3.at[(k - 1,) + s], device(to, c))
        return where

    def scatter4(parts, where, i):
        arrived(where)
        for part, col, n in parts:
            axis, rest, left = others(part, 2)
            s = (slice(None), pl.ds(col, n))
            t = S2[(me[axis],) + s].astype(F32)
            for k in range(3):
                t = t + R3[(k,) + s].astype(F32)
            KEEP[:, s[1]] = t[0:8, :] * c0 + t[8:16, :] * c1
            FSEND[:, s[1]] = t[0:8, :] * c1 + t[8:16, :] * c0
        s = columns(parts)
        copy = remote(FSEND.at[:, s], FRECV.at[:, s], ex_s.at[7 + i], ex_r.at[7 + i], sibling)
        copy.start()
        return copy

    def halves(col, n):
        keep = KEEP[:, col : col + n]
        got = FRECV[:, col : col + n]
        return keep * c0 + got * c1, keep * c1 + got * c0

    def finish(copy, first, last, where, i):
        copy.wait_recv()
        if first == OVEC:
            lo, hi = halves(VTILE, 128)
            PACK[:, OVEC:OK] = lo + hi
        for at, col in where:
            if col in (CQ, CK):
                lo, hi = halves(col, 512)
                PACK[:, at : at + 512] = lo
                PACK[:, at + 512 : at + 1024] = hi
            else:
                lo, hi = halves(col, WIDE)
                moved = pltpu.roll(jnp.concatenate([hi, jnp.zeros((8, 128), F32)], axis=1), 96, 1)
                first96 = lax.broadcasted_iota(jnp.int32, (8, 128), 1) < 96
                PACK[:, at : at + 768] = lo[:, 0:768]
                PACK[:, at + 768 : at + 896] = jnp.where(first96, lo[:, 768:896], moved[:, 0:128])
                PACK[:, at + 896 : at + 1792] = moved[:, 128:1024]
        out = pltpu.make_async_copy(PACK.at[:, first:last], pack_ref.at[:, first:last], loc.at[15 + i])
        out.start()
        return copy, out

    def emit_hidden(at, w, r):
        GGL[:, at : at + w] = (r * ACT[:, at : at + w]).astype(BF16)
        GUL[:, at : at + w] = (r * BCT[:, at : at + w]).astype(BF16)

    grad(TT, HID, CMD)
    r_down = scatter0(DOWN)
    fwd(G, CMD, WIDE, emit_hidden)
    transpose(SEC, TT)
    grad(TT, GGL, CMG)
    e_mid.wait_send()

    def second_body(i):
        r = mm_nt(GGL[...], wrows(i, CMG, WIDE)) + mm_nt(GUL[...], wrows(i, CMU, WIDE))
        s = pl.ds(pl.multiple_of(i * 256, 256), 256)
        GM[:, s] = r
        SB[:, s] = r.astype(BF16)
        remote(SB.at[:, s], RB2.at[:, s], ex_s.at[5], ex_r.at[5], sibling).start()

    loop(4, second_body)
    e_sec = remote(SB, RB2, ex_s.at[5], ex_r.at[5], sibling)
    grad(TT, GUL, CMU)
    r_mlp = scatter0(MLP)
    r_down = scatter1(DOWN, r_down)
    e_sec.wait_recv()

    def norm_back(gs, v, gain, at, which):
        rstd = STAT[which + 1, at, 0:1]
        xh = (v - STAT[which, at, 0:1]) * rstd
        gx = gs * gain
        m0 = jnp.mean(gx, axis=-1, keepdims=True)
        m1 = jnp.mean(gx * xh, axis=-1, keepdims=True)
        return rstd * (gx - m0 - xh * m1), jnp.sum(gs * xh, axis=0, keepdims=True), jnp.sum(gs, axis=0, keepdims=True)

    def ln2_back(i):
        gs = GM[rows(i), :] + RB2[rows(i), :].astype(F32)
        part, ggain, gbias = norm_back(gs, MID[rows(i), :], gain2, rows(i), 2)
        gm = G[rows(i), :].astype(F32) + part
        GM[rows(i), :] = gm
        GML[rows(i), :] = gm.astype(BF16)
        mine = (i // 4 == c).astype(F32)
        VA[2:3, :] += ggain * mine
        VA[3:4, :] += gbias * mine

    loop(8, ln2_back)
    transpose(GML, TT)
    grad(TT, GATED, CO)

    def emit_gated(at, w, r):
        ACT[:, at : at + w] = r

    fwd(GML, CO, WIDE, emit_gated)
    r_out = scatter0(OUT)

    def group_back(i):
        gr = ACT[rows(i), :]
        z = GATE[rows(i), :]
        sg = jax.nn.sigmoid(z)
        grp = GRP[rows(i), :]
        GGP[rows(i), :] = (gr * (sg * (1.0 + z * (1.0 - sg))) * grp).astype(BF16)
        gg = gr * (z * sg)
        gmx = RSTD[rows(i), :] * (gg - heads_mean(gg) - grp * heads_mean(gg * grp))
        GMX[rows(i), :] = jnp.where(real, gmx, 0.0).astype(BF16)

    loop(8, group_back)
    r_mlp = scatter1(MLP, r_mlp)
    transpose(GMX, VT)
    u_sent()
    for hh in range(2):
        r = mm(VT[VH * hh : VH * (hh + 1), :], QS[:, 256 * hh : 256 * (hh + 1)])
        UT[VH * hh : VH * (hh + 1), :] = r.astype(BF16)
    c_middle, c_finish, c_sent = states(UT, 8, True)
    wide = lax.broadcasted_iota(jnp.int32, (256, 512), 1)
    windows = (slice(0, 512), slice(384, 896))

    def window(ref, hh):
        a = ref[:, windows[hh]]
        keep = wide < VH if hh == 0 else wide >= VH - 384
        return jnp.where(keep, a, jnp.zeros_like(a))

    def spots(hh, offset, sign):
        spot = lax.broadcasted_iota(jnp.int32, (256, 128), 0).astype(F32)
        return jnp.exp((spot * sign + offset) * lg[hh])

    def unrotated(dst, src, hh, cross, offset, sign, scale):
        sc = spots(hh, offset, sign)
        co, si = COS[...], SIN[...]
        a, b = slice(256 * hh, 256 * hh + 128), slice(256 * hh + 128, 256 * hh + 256)
        u = (src[:, a] + cross[:, :128] * sc) * scale
        z = (src[:, b] + cross[:, 128:] * sc) * scale
        dst[:, a] = (u * co + z * si).astype(BF16)
        dst[:, b] = (z * co - u * si).astype(BF16)

    gvi = []
    for hh in range(2):
        h = slice(256 * hh, 256 * (hh + 1))
        gm = window(GMX, hh)
        vw = V[:, windows[hh]]
        graw = (mm_nt(gm, vw) * MASK[hh]).astype(BF16)
        ACT[:, h] = mm(graw, K[:, h])
        BCT[:, h] = mm(graw.T, Q[:, h])
        gvi.append(mm(WT[hh].T, gm))
        unrotated(GQ, ACT, hh, mm(gm, CT[windows[hh], :]), 1.0, 1.0, 1.0)
    join(MIX, gvi[0], gvi[1])
    grad(NORMT, GGP, CG)
    grad(NORMT, GQ, CQ)
    r_down = scatter2(DOWN, r_down)
    r_qg = scatter0(QG)
    c_middle(0, 1)

    def down_body(i):
        r = mm_nt(HID[...], wrows(i, CMD, WIDE))
        s = pl.ds(pl.multiple_of(i * 256, 256), 256)
        OWN1[:, s] = r[0:128] * c0 + r[128:256] * c1
        SBO[:, s] = (r[0:128] * c1 + r[128:256] * c0).astype(BF16)

    loop(4, down_body)
    e_out = remote(SBO, RBO, ex_s.at[4], ex_r.at[4], sibling)
    e_out.start()
    c_middle(2, 3)
    r_mlp = scatter2(MLP, r_mlp)
    e_out.wait_recv()
    OUTV[0] = (MID[rows_own, :] + OWN1[...] + RBO[...].astype(F32)).astype(BF16)
    put_out = pltpu.make_async_copy(OUTV.at[0], out_ref, loc.at[13])
    put_out.start()

    def normed_first(i):
        r = mm_nt(GQ[...], wrows(i, CQ, 512)) + mm_nt(GGP[...], wrows(i, CG, WIDE))
        MID[:, pl.ds(pl.multiple_of(i * 256, 256), 256)] = r

    loop(4, normed_first)
    r_qg = scatter1(QG, r_qg)
    c_finish(GUT)

    gvs = []
    for hh in range(2):
        h = slice(256 * hh, 256 * (hh + 1))
        unrotated(GK, BCT, hh, mm(window(V, hh), GUT[windows[hh], :]), 255.0, -1.0, 0.0625)
        gvs.append(mm_nt(KW[:, h], GUT[windows[hh], :]))
    join(ACT, gvs[0], gvs[1])
    GV[...] = (MIX[...] + ACT[...]).astype(BF16)
    grad(NORMT, GV, CV)
    grad(NORMT, GK, CK)
    r_kv = scatter0(KV_EARLY, stage(RB1.at[:, :, :, :, columns(KV)]))
    e_out.wait_send()

    def normed_body(i):
        s = pl.ds(pl.multiple_of(i * 256, 256), 256)
        r = MID[:, s] + mm_nt(GK[...], wrows(i, CK, 512)) + mm_nt(GV[...], wrows(i, CV, WIDE))
        OWN2[:, s] = r[0:128] * c0 + r[128:256] * c1
        SBO[:, s] = (r[0:128] * c1 + r[128:256] * c0).astype(BF16)
        remote(SBO.at[:, s], RB3.at[:, s], ex_s.at[6], ex_r.at[6], sibling).start()

    loop(4, normed_body)
    e_norm = remote(SBO, RB3, ex_s.at[6], ex_r.at[6], sibling)
    r_out = scatter1(OUT, r_out)
    e_norm.wait_recv()

    def ln1_back(i):
        at = pl.ds(pl.multiple_of(c * 128 + i * 32, 32), 32)
        gs = OWN2[rows(i), :] + RB3[rows(i), :].astype(F32)
        part, ggain, gbias = norm_back(gs, X[at, :].astype(F32), gain1, at, 0)
        OUTV[1, rows(i), :] = (GM[at, :] + part).astype(BF16)
        VA[0:1, :] += ggain
        VA[1:2, :] += gbias

    loop(4, ln1_back)
    put_gin = pltpu.make_async_copy(OUTV.at[1], gin_ref, loc.at[14])
    put_gin.start()
    vectors = jnp.concatenate([jnp.zeros((96, 1024), F32), VA[...], jnp.zeros((24, 1024), F32)], axis=0).T
    tile = slice(VTILE, VTILE + 128)
    Gd[:, :, :, :, tile] = (
        Gd[:, :, :, :, tile].astype(F32) + vectors.reshape(4, 4, 4, 16, 128)
    ).astype(BF16)
    r_vec = scatter0(KV_LATE, r_kv[1])
    r_kv = scatter1(KV_EARLY, r_kv)
    scatter1(KV_LATE, r_vec)
    r_qg = scatter2(QG, r_qg)
    r_out = scatter2(OUT, r_out)
    r_kv = scatter2(KV, r_kv)
    r_mlp = scatter3(MLP, r_mlp)
    r_qg = scatter3(QG, r_qg)
    r_down = scatter3(DOWN, r_down)
    r_out = scatter3(OUT, r_out)
    r_kv = scatter3(KV, r_kv)
    f_out = scatter4(OUT, r_out, 2)
    f_down = scatter4(DOWN, r_down, 0)
    f_mlp = scatter4(MLP, r_mlp, 1)
    f_qg = scatter4(QG, r_qg, 3)
    f_out = finish(f_out, OO, OMG, ((OO, CO),), 2)
    f_down = finish(f_down, OMD, OTOTAL, ((OMD, CMD),), 0)
    f_mlp = finish(f_mlp, OMG, OMD, ((OMG, CMG), (OMU, CMU)), 1)
    f_kv = scatter4(KV, r_kv, 4)
    f_qg = finish(f_qg, OQ, OO, ((OQ, CQ), (OG, CG)), 3)
    f_kv = finish(f_kv, 0, OQ, ((OK, CK), (OV, CV)), 4)
    c_sent()
    put_out.wait()
    put_gin.wait()
    for where in pending:
        remote(where[2], where[2], where[0], where[1], sibling).wait_send()
    for copy in (e_pack, e_x, e_g, e_sec, e_norm):
        copy.wait_send()
    for copy, out in (f_down, f_mlp, f_out, f_qg, f_kv):
        copy.wait_send()
        out.wait()


def scratch():
    def b(*shape):
        return pltpu.VMEM(shape, BF16)

    def f(*shape):
        return pltpu.VMEM(shape, F32)

    def sem(n):
        return pltpu.SemaphoreType.DMA((n,))

    return [
        b(4, 4, 4, 16, TOTAL), b(4, 4, 4, 16, TOTAL), b(2, 2, 4, 16, TOTAL), b(2, 4, 4, 16, TOTAL),
        b(3, 4, 16, TOTAL), b(3, 16, TOTAL),
        b(256, 1024), b(256, 1024), f(8, 1792), b(2, 8, 1024), b(6, 8, 1728), f(8, 128), f(8, OTOTAL),
        b(2, 128, 1024), b(16, TOTAL), b(2, 16, TOTAL), f(8, 1024), f(8, 1024),
        f(256, 128), f(256, 128), f(4, 256, 128),
        b(256, 1024), b(1024, 256), b(1024, 256), b(256, 512), b(256, 512), b(256, 512), b(256, 512),
        b(256, WIDE), b(256, WIDE), f(256, WIDE), b(2, 256, 256), f(2, 256, 256), f(256, WIDE), f(256, WIDE),
        b(REAL, 256), b(REAL, 256), b(3, REAL, 256), b(WIDE, 256), b(WIDE, 256),
        b(256, WIDE), f(256, 1024), b(256, 1024), b(256, 1024), b(128, 1024), b(128, 1024), f(128, 1024),
        b(256, 1024), b(128, 1024), f(128, 1024),
        b(256, 1024), f(256, WIDE), f(256, WIDE), b(256, WIDE), b(256, WIDE), b(256, WIDE),
        f(256, 1024), b(256, WIDE), b(256, 512), b(256, 512), b(256, WIDE),
        f(8, TOTAL), f(8, TOTAL), f(8, TOTAL),
        sem(44), sem(44), sem(16), sem(16), sem(12), sem(12), sem(20),
    ]


def per_device(
    inputs, cotangent, ln1_gain, ln1_bias, w_query, w_key, w_value, w_gate, w_out,
    ln2_gain, ln2_bias, w_mlp_gate, w_mlp_up, w_mlp_down,
):
    cosine, sine = tables()
    vectors = jnp.stack([ln1_gain, ln1_bias, ln2_gain, ln2_bias]).astype(F32)
    vectors = jnp.pad(vectors, ((0, 4), (0, 120)))
    out, gin, pack = pl.pallas_call(
        kernel,
        out_shape=[
            jax.ShapeDtypeStruct((128, 1024), BF16), jax.ShapeDtypeStruct((128, 1024), BF16),
            jax.ShapeDtypeStruct((8, OTOTAL), F32),
        ],
        in_specs=[pl.BlockSpec(memory_space=pl.ANY)] * 13,
        out_specs=[pl.BlockSpec(memory_space=pl.ANY)] * 3,
        scratch_shapes=scratch(),
        compiler_params=pltpu.CompilerParams(
            collective_id=0, has_side_effects=True, vmem_limit_bytes=64 << 20
        ),
        name="block",
    )(
        inputs[0], cotangent[0], vectors, w_query, w_key, w_value, w_gate, w_out.T,
        w_mlp_gate, w_mlp_up, w_mlp_down.T, jnp.asarray(cosine), jnp.asarray(sine),
    )
    gv, gg, go, gmg, gmu, gmd = (pack[:, at : at + 1728] for at in (OV, OG, OO, OMG, OMU, OMD))
    vec = [pack[:, OVEC + 96 + i] for i in range(4)]
    return (
        out[None], gin[None], vec[0], vec[1], pack[:, OQ : OQ + 1024], pack[:, OK : OK + 1024], gv, gg, go.T,
        vec[2], vec[3], gmg, gmu, gmd.T,
    )


def solution(mesh):
    both = ("dp", "seq")
    row, col, vec, tokens = P(both, None), P(None, both), P(both), P("dp", "seq", None)
    return jax.shard_map(
        per_device,
        mesh=mesh,
        in_specs=(tokens, tokens, vec, vec, row, row, row, row, col, vec, vec, row, row, col),
        out_specs=(tokens, tokens, vec, vec, row, row, row, row, col, vec, vec, row, row, col),
        check_vma=False,
    )
```

profile of v0, /device:TPU:1, one launch (start us, length us, event | category | flops | bytes accessed | tf_op | source)
XLA Modules:
  0.0 145.0 jit_solution(17260650043647459881)
XLA Ops:
  0.6 0.0 copy-start.5
  0.7 0.0 copy-start.2
  0.7 0.0 copy-start.3
  0.7 0.0 copy-start.4
  0.7 0.6 copy-done.5
  1.3 0.0 copy-done.2
  1.3 0.0 copy-done.3
  1.3 0.0 copy-done.4
  1.3 0.6 fusion.9.vec_in
  2.0 136.6 %block.1 = (bf16[128,1024]{1,0:T(8,128)(2,1)}, bf16[128,1024]{1,0:T(8,128)(2,1)}, f32[8,12928]{1,0:T(8,128)}) custom-call(bf16[128,1024]{1,0:T(8,128)(2,1)} %bitcast.14, bf16[128,1024]{1,0:T(8,128)(2,1)} %bitcast.15, f32[8,128]{1,0:T(8,128)} %fusion.9.vec_in, bf16[8,1024]{1,0:T(8,128)(2,1)} %wq_in.1, bf16[8,1024]{1,0:T(8,128)(2,1)} %wk_in.1, ...), custom_call_target="tpu_custom_call" | custom-call | tf_op jit(solution)/shard_map/block/pallas_call | solution.py:869
  138.5 1.6 %slice_reduce_fusion = (f32[8]{0:T(128)}, f32[8]{0:T(128)}, f32[8]{0:T(128)}, f32[8]{0:T(128)}) fusion(f32[8,12928]{1,0:T(8,128)} %get-tuple-element.19), kind=kLoop, calls=%fused_computation.9 | loop fusion | bytes 256 | tf_op jit(solution)/shard_map/slice | solution.py:887
  140.1 1.4 fusion.13
  141.5 0.0 copy-start.1
  141.5 1.7 %slice_bitcast_fusion = (f32[1728,8]{0,1:T(8,128)}, f32[1728,8]{0,1:T(8,128)}, f32[8,1728]{1,0:T(8,128)}, f32[8,1728]{1,0:T(8,128)}, f32[8,1728]{1,0:T(8,128)}, /*index=5*/f32[8,1728]{1,0:T(8,128)}) fusion(f32[8,12928]{1,0:T(8,128)} %get-tuple-element.19), kind=kLoop, calls=%fused_computation | loop fusion | bytes 663552 | tf_op jit(solution)/shard_map/transpose | solution.py:890
  143.2 0.0 copy-done.1
  143.2 0.0 copy-start
  143.2 0.7 copy.32
  143.9 0.3 copy-done
  144.3 0.7 copy.33
Async XLA Ops:
  0.6 0.7 copy-start.5
  0.7 0.7 copy-start.2
  0.7 0.7 copy-start.3
  0.7 0.7 copy-start.4
  141.5 1.7 %copy-start.1 = (bf16[128,1024]{1,0:T(8,128)(2,1)S(1)}, bf16[128,1024]{1,0:T(8,128)(2,1)}, u32[]{:S(2)}) copy-start(bf16[128,1024]{1,0:T(8,128)(2,1)} %get-tuple-element.17) | copy-start | bytes 786436
  143.2 1.0 copy-start
where the time goes:
time: 145 us
  Pallas kernels  137 us (94%)
  local copies, waits for them, and re-layouts  7.11 us (5%)
    pallas_call x1, Pallas kernels, per_device(): pl.pallas_call(kernel, out_shape=[jax.ShapeDtypeStruct((128, 1024), BF16)...  137 us

commit v1 on v0

v1 whole, which is shorter than its diff:
```python
import functools

import jax
import jax.numpy as jnp
import numpy as np
from jax import lax
from jax.experimental import pallas as pl
from jax.experimental.pallas import tpu as pltpu
from jax.sharding import PartitionSpec as P

MESH = pl.DeviceIdType.MESH
F32 = jnp.float32
BF16 = jnp.bfloat16
EPS = 1e-05
VH = 432

CK, CV, CQ, CG, CO, CMG, CMU, CMD, TOTAL = 0, 512, 1408, 1920, 2816, 3712, 4608, 5504, 6400
WIDE = 896
REAL = 864
VTILE = CV + 768


def cut(start, *tiles):
    parts = []
    for part, n in enumerate(tiles):
        parts.append((part, start, 128 * n))
        start += 128 * n
    return tuple(parts)


GATHERS = (
    cut(CK, 4, 3, 4), cut(CQ, 4, 4, 3), cut(CO, 2, 2, 3), cut(CMG, 6, 2, 6), cut(CMD, 3, 2, 2),
)
KV = cut(CK, 4, 4, 3)
KV_EARLY, KV_LATE = cut(CK, 4, 4, 2), ((2, VTILE, 128),)
QG, OUT, MLP, DOWN = cut(CQ, 5, 3, 3), cut(CO, 1, 2, 4), cut(CMG, 6, 2, 6), cut(CMD, 3, 3, 1)
FORWARD_GATHERS = (1, 2, 3, 4,)
PIECES = ((slice(0, 224), 0), (slice(224, 432), 0), (slice(432, 656), 1), (slice(656, 864), 1))
ORDERS = (("x", "y", "z"), ("y", "z", "x"), ("z", "x", "y"))
ZYX = ("z", "y", "x")


def tables():
    half = 128
    inverse = np.power(10000.0, -np.arange(half, dtype=np.float64) / half)
    angles = np.arange(1024, dtype=np.float64)[:, None] * inverse[None, :]
    return (
        np.cos(angles).astype(np.float32).reshape(4, 256, half),
        np.sin(angles).astype(np.float32).reshape(4, 256, half),
    )


def mm(a, b):
    return lax.dot_general(a, b, (((1,), (0,)), ((), ())), preferred_element_type=F32)


def mm_nt(a, b):
    return lax.dot_general(a, b, (((1,), (1,)), ((), ())), preferred_element_type=F32)


def loop(n, body):
    def step(i, carry):
        body(i)
        return carry

    lax.fori_loop(0, n, step, 0)


def each(n, body):
    for i in range(n):
        body(i)


def kernel(
    gain1_in, bias1_in, gain2_in, bias2_in, x_in, g_in, wq_in, wk_in, wv_in, wg_in, wo_in, wmg_in, wmu_in, wmd_in,
    cos_in, sin_in, out_ref, gin_ref, vec_ref, gq_ref, gk_ref, gv_ref, gg_ref, go_ref, gmg_ref, gmu_ref, gmd_ref,
    *scratch,
):
    (
        W, Gd, RA, RB1, R2A, R2B, R2C, R3, X, G, WS, IN8, INW, INV, OUT8, OUTW, OUTVEC, OUTV, PSEND, PRECV, VEC, VA, COS, SIN, STAT,
        NORM, NORMT, TT, Q, QS, K, KW, V, GGP, GATE, WT, MASK, MIX, GRP,
        UT, TOT, STATES, CT, GUT, GATED, MID, SB, RB, SBO, RBO, OWN1, RB2, RB3, OWN2,
        SEC, ACT, BCT, HID, GGL, GUL, GM, GMX, GQ, GK, GV, FSEND, FRECV, KEEP,
        way_s, way_r, st_s, st_r, ex_s, ex_r, loc,
    ) = scratch
    S1, S2, VT, RSTD, GML = RB1.at[0], R2B.at[0], TT.at[0:WIDE], MIX, SEC
    dp = lax.axis_index("dp")
    sq = lax.axis_index("seq")
    me = {"z": dp // 4, "y": dp % 4, "x": sq // 2}
    c = sq % 2
    c0 = (c == 0).astype(F32)
    c1 = (c == 1).astype(F32)

    def shifted(axis, k):
        p = dict(me)
        p[axis] = (me[axis] + k) % 4
        return p

    def device(p, core):
        return (p["z"] * 4 + p["y"], p["x"] * 2 + core)

    sibling = device(me, 1 - c)

    def remote(src, dst, ss, rs, dev):
        return pltpu.make_async_remote_copy(
            src_ref=src, dst_ref=dst, send_sem=ss, recv_sem=rs, device_id=dev, device_id_type=MESH
        )

    rows_own = pl.ds(pl.multiple_of(c * 128, 128), 128)
    rows_sib = pl.ds(pl.multiple_of((1 - c) * 128, 128), 128)
    fetch = [
        pltpu.make_async_copy(src, dst, loc.at[i])
        for i, (src, dst) in enumerate(
            (
                (wq_in, IN8.at[0]), (wk_in, IN8.at[1]), (wv_in, INW.at[0]), (wg_in, INW.at[1]),
                (wo_in, INW.at[2]), (wmg_in, INW.at[3]), (wmu_in, INW.at[4]), (wmd_in, INW.at[5]),
                (x_in, X.at[rows_own, :]), (g_in, G.at[rows_own, :]),
                (cos_in.at[me["x"]], COS), (sin_in.at[me["x"]], SIN),
            )
        )
    ]
    for copy in fetch:
        copy.start()
    barrier = pltpu.get_barrier_semaphore()
    pl.semaphore_signal(barrier, inc=1, device_id=sibling, device_id_type=MESH)
    for axis in ZYX:
        for k in (1, 2, 3):
            pl.semaphore_signal(
                barrier, inc=1, device_id=device(shifted(axis, k), c), device_id_type=MESH
            )

    def put(ref, col, own):
        both = jnp.concatenate([own * c0, own * c1], axis=0)
        ref[:, col : col + own.shape[1]] = both.astype(BF16)

    def pack(col, h0, h1):
        put(PRECV.at[0], col, h0 * c0 + h1 * c1)
        put(PSEND, col, h0 * c1 + h1 * c0)

    def pack_square(i, col):
        w = IN8[i].astype(F32)
        pack(col, w[:, :512], w[:, 512:])

    def pack_wide(i, col):
        lane = lax.broadcasted_iota(jnp.int32, (8, WIDE), 1)
        WS[:, 1664:1792] = jnp.zeros((8, 128), F32)
        WS[:, :1728] = INW[i].astype(F32)
        h0 = jnp.where(lane < REAL, WS[:, :WIDE], 0.0)
        h1 = pltpu.roll(WS[:, 768:1792], 1024 - 96, 1)[:, :WIDE]
        h1 = jnp.where(lane < REAL, h1, 0.0)
        if col == CV:
            v = jnp.concatenate([INV[...], jnp.zeros((120, 128), F32)], axis=0).T
            v = pltpu.roll(v[0:8, :], 96, 1)
            v = jnp.concatenate([jnp.zeros((8, 768), F32), v], axis=1)
            h0 = h0 + v
            h1 = h1 + v
        pack(col, h0, h1)

    def exchange(first, last, i):
        s = pl.ds(first, last - first)
        copy = remote(PSEND.at[:, s], PRECV.at[1, :, s], ex_s.at[i], ex_r.at[i], sibling)
        copy.start()
        return copy

    def assemble(copy, first, last):
        copy.wait_recv()
        for col in range(first, last, 640):
            s = pl.ds(col, min(640, last - col))
            W[me["z"], me["y"], me["x"], :, s] = (
                PRECV[0, :, s].astype(F32) + PRECV[1, :, s].astype(F32)
            ).astype(BF16)

    INV[...] = jnp.zeros_like(INV)
    for i, ref in enumerate((gain1_in, bias1_in, gain2_in, bias2_in)):
        INV[i : i + 1, 0:8] = ref[...].astype(F32)
    for copy in fetch[:8]:
        copy.wait()
    pack_square(1, CK)
    pack_wide(0, CV)
    pl.semaphore_wait(barrier, 10)
    e_first = exchange(0, CQ, 0)
    pack_square(0, CQ)
    for i, col in enumerate((CG, CO, CMG, CMU, CMD)):
        pack_wide(i + 1, col)
    e_rest = exchange(CQ, TOTAL, 12)
    fetch[8].wait()
    e_x = remote(X.at[rows_own, :], X.at[rows_own, :], ex_s.at[1], ex_r.at[1], sibling)
    e_x.start()
    fetch[9].wait()
    e_g = remote(G.at[rows_own, :], G.at[rows_own, :], ex_s.at[2], ex_r.at[2], sibling)
    e_g.start()

    pending = []
    count = [0]

    def stage(total):
        count[0] += 1
        return way_s.at[count[0] - 1], way_r.at[count[0] - 1], total

    def send(where, src, dst, dev):
        remote(src, dst, where[0], where[1], dev).start()

    def arrived(where):
        ss, rs, total = where
        remote(total, total, ss, rs, sibling).wait_recv()
        pending.append(where)

    def columns(parts):
        return pl.ds(parts[0][1], sum(n for _, _, n in parts))

    def gather(group, phase, forward=False):
        s = columns(GATHERS[group])
        halves = phase == 2 or (phase == 1 and group in FORWARD_GATHERS)
        if phase == 1:
            where = stage(W.at[0, 0 : 1 if forward else 2 if halves else 3, :, :, s])
        else:
            where = stage(W.at[0, :, :, :, s] if forward else W.at[0:2, :, :, :, s])
        gather_parts(where, GATHERS[group], phase, halves, forward)
        return where

    def gather_parts(where, parts, phase, halves, forward):
        for part, col, n in parts:
            order = ORDERS[part]
            axis = order[phase]
            for i, k in enumerate((1, 3) if halves else (1, 2, 3)):
                idx = {a: me[a] for a in ZYX}
                for a in order[:phase]:
                    idx[a] = slice(None)
                if forward:
                    idx[axis] = (me[axis] - k) % 4
                    idx[[a for a in ZYX if a in order[:phase]][0]] = pl.ds(2 * i, 2)
                src = W.at[tuple(idx[a] for a in ZYX) + (slice(None), pl.ds(col, n))]
                send(where, src, src, device(shifted(axis, k), c))

    def first_phase(groups, first, last):
        where = stage(W.at[0, 0, 0:3, :, first:last])
        for g in groups:
            gather_parts(where, GATHERS[g], 0, False, False)
        return where

    assemble(e_first, 0, CQ)
    p1 = {0: first_phase((0,), 0, CQ)}
    assemble(e_rest, CQ, TOTAL)
    p1[1] = first_phase((1, 2, 3, 4), CQ, TOTAL)
    p2, p3, p4, p5 = {}, {}, {}, {}
    waited = []

    def w1(g):
        at = min(g, 1)
        if at not in waited:
            waited.append(at)
            arrived(p1[at])
        p2[g] = gather(g, 1)

    def w2(g):
        if g in FORWARD_GATHERS:
            arrived(p2[g])
            p3[g] = gather(g, 1, True)

    def w3(g):
        arrived(p3[g] if g in FORWARD_GATHERS else p2[g])
        p4[g] = gather(g, 2)

    def w4(g):
        arrived(p4[g])
        p5[g] = gather(g, 2, True)

    def w5(g):
        arrived(p5[g])

    def wcols(col, n):
        return W[:, :, :, :, col : col + n].reshape(1024, n)

    def wrows(i, col, n):
        return W[i, :, :, :, col : col + n].reshape(256, n)

    def fwd(a, col, n, emit):
        for at in range(0, n, 256):
            w = min(256, n - at)
            emit(at, w, mm(a[...], wcols(col + at, w)))

    def grad(at, b, col):
        n = b.shape[1]

        def body(i):
            r = mm(at[pl.ds(i * 256, 256), :], b[...])
            Gd[i, :, :, :, col : col + n] = r.astype(BF16).reshape(4, 4, 16, n)

        each(4, body)

    def rows(i, n=64):
        return pl.ds(pl.multiple_of(i * n, n), n)

    lanes = lax.broadcasted_iota(jnp.int32, (64, WIDE), 1)
    in0 = lanes < VH
    in1 = (lanes >= VH) & (lanes < REAL)
    real = lanes < REAL

    def log_gamma(hh):
        g0 = float(np.log(1.0 - 2.0 ** (-5.0 - hh)))
        g1 = float(np.log(1.0 - 2.0 ** (-7.0 - hh)))
        return jnp.where(c == 0, jnp.float32(g0), jnp.float32(g1))

    lg = [log_gamma(0), log_gamma(1)]

    def mask_body(i):
        ii = lax.broadcasted_iota(jnp.int32, (64, 256), 0) + i * 64
        jj = lax.broadcasted_iota(jnp.int32, (64, 256), 1)
        d = (ii - jj).astype(F32)
        for hh in range(2):
            MASK[hh, rows(i), :] = jnp.where(d >= 0, jnp.exp(jnp.maximum(d, 0.0) * lg[hh]), 0.0)

    loop(4, mask_body)
    VA[...] = jnp.zeros_like(VA)
    e_x.wait_recv()
    e_g.wait_recv()

    def norm(v):
        mean = jnp.mean(v, axis=-1, keepdims=True)
        center = v - mean
        spread = jnp.mean(center * center, axis=-1, keepdims=True)
        rstd = lax.rsqrt(spread + EPS)
        return center * rstd, rstd, mean

    def ln1_stats(i):
        xh, rstd, mean = norm(X[rows(i), :].astype(F32))
        GM[rows(i), :] = xh
        STAT[0, rows(i), :] = jnp.broadcast_to(mean, (64, 128))
        STAT[1, rows(i), :] = jnp.broadcast_to(rstd, (64, 128))

    loop(4, ln1_stats)
    fetch[10].wait()
    fetch[11].wait()

    def transpose(src, dst):
        dst[...] = src[...].T

    def vector(i):
        return VEC[i : i + 1, :]

    def ln1():
        VEC[...] = wcols(VTILE, 128).astype(F32).T[96:104, :]
        gain1, bias1 = vector(0), vector(1)

        def ln1(i):
            NORM[rows(i), :] = (GM[rows(i), :] * gain1 + bias1).astype(BF16)

        loop(4, ln1)

    def rotated(dst, dst2, offset, sign, scale):
        def emit(at, w, r):
            hh = at // 256
            u, z = r[:, :128], r[:, 128:]
            co, si = COS[...], SIN[...]
            a0 = ((u * co - z * si) * scale).astype(BF16)
            a1 = ((u * si + z * co) * scale).astype(BF16)
            spot = lax.broadcasted_iota(jnp.int32, (256, 128), 0).astype(F32)
            sc = jnp.exp((spot * sign + offset) * lg[hh])
            dst[:, at : at + 128] = a0
            dst[:, at + 128 : at + 256] = a1
            dst2[:, at : at + 128] = (a0.astype(F32) * sc).astype(BF16)
            dst2[:, at + 128 : at + 256] = (a1.astype(F32) * sc).astype(BF16)

        return emit

    def emit_v(at, w, r):
        col = lax.broadcasted_iota(jnp.int32, (256, w), 1) + at
        V[:, at : at + w] = jnp.where(col < REAL, r, 0.0).astype(BF16)

    def kvu():
        fwd(NORM, CK, 512, rotated(K, KW, 255.0, -1.0, 0.0625))
        fwd(NORM, CV, WIDE, emit_v)
        transpose(V, VT)
        for hh in range(2):
            r = mm(VT[VH * hh : VH * (hh + 1), :], KW[:, 256 * hh : 256 * (hh + 1)])
            UT[VH * hh : VH * (hh + 1), :] = r.astype(BF16)

    def states(src, base, back):
        x = me["x"]
        near = dict(me, x=x + 1 - 2 * (x % 2))
        far = dict(me, x=3 - x)
        low = x < 2
        sends = (x != 0) if back else (x != 3)
        gets = (x != 1) if back else (x != 2)
        passes = ~low if back else low
        steps = []
        for i, (at, hh) in enumerate(PIECES):
            t = base + i
            slot = 1 if back else 0
            one = remote(src.at[at], STATES.at[slot, at], st_s.at[t], st_r.at[t], device(near, c))
            pl.when(sends)(one.start)
            steps.append(one)

        def second(i):
            at, hh = PIECES[i]
            t = base + 4 + i
            two = remote(TOT.at[at], STATES.at[2, at], st_s.at[t], st_r.at[t], device(far, c))

            def total():
                steps[i].wait_recv()
                own = src[at, :].astype(F32)
                got = STATES[slot, at, :].astype(F32)
                g = jnp.exp(256.0 * lg[hh])
                first = (x % 2 == 1) if back else (x % 2 == 0)
                TOT[at, :] = jnp.where(first, own * g + got, own + got * g).astype(BF16)
                two.start()

            pl.when(passes)(total)
            return two

        def finish(dst):
            dst[...] = jnp.zeros_like(dst)
            for i, two in enumerate(twos):
                at, hh = PIECES[i]
                g = jnp.exp(256.0 * lg[hh])

                def single():
                    dst[at, :] = STATES[slot, at, :]

                def double():
                    two.wait_recv()
                    dst[at, :] = STATES[2, at, :]

                def triple():
                    steps[i].wait_recv()
                    two.wait_recv()
                    total = STATES[2, at, :].astype(F32) * g
                    dst[at, :] = (total + STATES[slot, at, :].astype(F32)).astype(BF16)

                one, pair, three = (2, 1, 0) if back else (1, 2, 3)
                pl.when(x == one)(single)
                pl.when(x == pair)(double)
                pl.when(x == three)(triple)

        def sent():
            for one, two in zip(steps, twos):
                pl.when(sends)(one.wait_send)
                pl.when(passes)(two.wait_send)

        twos = []

        def middle(*pieces):
            twos.extend(second(i) for i in pieces)

        return middle, finish, sent

    def join(dst, h0, h1):
        pick = lax.broadcasted_iota(jnp.int32, (256, 128), 1) < VH - 384
        dst[:, 0:384] = h0[:, :384]
        dst[:, 384:512] = jnp.where(pick, h0[:, 384:512], h1[:, :128])
        dst[:, 512:896] = h1[:, 128:512]

    def qi():
        fwd(NORM, CQ, 512, rotated(Q, QS, 1.0, 1.0, 1.0))
        for hh in range(2):
            raw = mm_nt(Q[:, 256 * hh : 256 * (hh + 1)], K[:, 256 * hh : 256 * (hh + 1)])
            WT[hh] = (raw * MASK[hh]).astype(BF16)
        join(MIX, mm(WT[0], V[:, 0:512]), mm(WT[1], V[:, 384:896]))

    def emit_gate(at, w, r):
        GATE[:, at : at + w] = r

    def gate():
        fwd(NORM, CG, WIDE, emit_gate)

    def cross():
        join(GRP, mm_nt(QS[:, 0:256], CT[0:512, :]), mm_nt(QS[:, 256:512], CT[384:896, :]))

    def heads_mean(v):
        m0 = jnp.sum(jnp.where(in0, v, 0.0), axis=-1, keepdims=True) * (1.0 / VH)
        m1 = jnp.sum(jnp.where(in1, v, 0.0), axis=-1, keepdims=True) * (1.0 / VH)
        return jnp.where(in0, m0, m1)

    def group_norm(i):
        m = MIX[rows(i), :] + GRP[rows(i), :]
        center = m - heads_mean(m)
        rstd = lax.rsqrt(heads_mean(center * center) + EPS)
        grouped = jnp.where(real, center * rstd, 0.0)
        GRP[rows(i), :] = grouped
        RSTD[rows(i), :] = rstd
        gate = GATE[rows(i), :]
        GATED[rows(i), :] = (gate * jax.nn.sigmoid(gate) * grouped).astype(BF16)

    def gn():
        loop(4, group_norm)

    def out_body(i):
        r = mm_nt(GATED[...], wrows(i, CO, WIDE))
        s = pl.ds(i * 256, 256)
        MID[:, s] = r
        SB[:, s] = r.astype(BF16)
        remote(SB.at[:, s], RB.at[:, s], ex_s.at[3], ex_r.at[3], sibling).start()

    def out():
        each(4, out_body)

    e_mid = remote(SB, RB, ex_s.at[3], ex_r.at[3], sibling)

    def ln2():
        gain2, bias2 = vector(2), vector(3)

        def ln2_rows(i):
            m = X[rows(i), :].astype(F32) + MID[rows(i), :] + RB[rows(i), :].astype(F32)
            MID[rows(i), :] = m
            xh, rstd, mean = norm(m)
            STAT[2, rows(i), :] = jnp.broadcast_to(mean, (64, 128))
            STAT[3, rows(i), :] = jnp.broadcast_to(rstd, (64, 128))
            SEC[rows(i), :] = (xh * gain2 + bias2).astype(BF16)

        e_mid.wait_recv()
        loop(4, ln2_rows)

    def emit_act(at, w, r):
        ACT[:, at : at + w] = r

    def emit_bct(at, w, r):
        BCT[:, at : at + w] = r

    def gelu_rows(i):
        g = ACT[rows(i), :]
        u = BCT[rows(i), :]
        cdf = 0.5 * (1.0 + lax.erf(g * 0.7071067811865476))
        ge = g * cdf
        HID[rows(i), :] = (ge * u).astype(BF16)
        BCT[rows(i), :] = ge
        ACT[rows(i), :] = (cdf + g * jnp.exp(-0.5 * g * g) * 0.3989422804014327) * u

    def mlp():
        fwd(SEC, CMG, WIDE, emit_act)
        fwd(SEC, CMU, WIDE, emit_bct)

    def gelu():
        loop(4, gelu_rows)

    def place(axes, where):
        return tuple(where.get(a, slice(None)) for a in axes)

    def others(part, phase):
        order = ORDERS[part][::-1]
        return order[phase], [a for a in ZYX if a not in order[: phase + 1]], [a for a in ZYX if a not in order[:phase]]

    def scatter0(parts, late=None):
        s = columns(parts)
        early = stage(RA.at[:, :, :, :, s])
        late = late or stage(RB1.at[:, :, :, :, s])
        for where in (early, late):
            for part, col, n in parts:
                axis, rest, left = others(part, 0)
                s = (slice(None), pl.ds(col, n))
                for i, k in enumerate((1, 3)):
                    dev = device(shifted(axis, k), c)
                    if where is early:
                        src = Gd.at[place(left, {axis: (me[axis] + 2) % 4, rest[0]: pl.ds(2 * i, 2)}) + s]
                        send(where, src, RA.at[(i, slice(None), slice(None)) + s], dev)
                    else:
                        near = pl.ds(2 - 2 * i, 2)
                        src = Gd.at[place(left, {axis: (me[axis] + k) % 4, rest[0]: near}) + s]
                        send(where, src, RB1.at[(i, near, slice(None)) + s], dev)
        return early, late

    def scatter1(parts, where):
        early, late = where
        arrived(early)
        for part, col, n in parts:
            axis, rest, left = others(part, 0)
            s = (slice(None), pl.ds(col, n))
            for i, k in enumerate((1, 3)):

                def body(j):
                    own = Gd[place(left, {axis: (me[axis] + k) % 4, rest[0]: 2 * i + j}) + s]
                    at = (i, j, slice(None)) + s
                    RA[at] = (own.astype(F32) + RA[at].astype(F32)).astype(BF16)

                loop(2, body)
                src = RA.at[(i, slice(None), slice(None)) + s]
                dst = RB1.at[(i, pl.ds(2 * i, 2), slice(None)) + s]
                send(late, src, dst, device(shifted(axis, k), c))
        return late

    def scatter2(parts, late):
        arrived(late)
        direct = parts is KV
        if direct:
            early = stage(R2C.at[:, :, :, columns(parts)])
        else:
            early, late = stage(R2A.at[:, :, :, columns(parts)]), stage(R2B.at[:, :, :, columns(parts)])
        for part, col, n in parts:
            axis, rest, left = others(part, 0)
            s = (slice(None), pl.ds(col, n))

            def body(j):
                own = Gd[place(left, {axis: me[axis], rest[0]: j}) + s].astype(F32)
                at = (j, slice(None)) + s
                RB1[(0,) + at] = (own + RB1[(0,) + at].astype(F32) + RB1[(1,) + at].astype(F32)).astype(BF16)

            loop(4, body)
            axis, rest, left = others(part, 1)
            if direct:
                for k in (1, 2, 3):
                    to = shifted(axis, k)
                    src = S1.at[place(left, {axis: to[axis]}) + s]
                    send(early, src, R2C.at[(k - 1, slice(None)) + s], device(to, c))
                continue
            for i, k in enumerate((1, 3)):
                dev = device(shifted(axis, k), c)
                src = S1.at[place(left, {axis: (me[axis] + 2) % 4, rest[0]: pl.ds(2 * i, 2)}) + s]
                send(early, src, R2A.at[(i, slice(None)) + s], dev)
                near = pl.ds(2 - 2 * i, 2)
                src = S1.at[place(left, {axis: (me[axis] + k) % 4, rest[0]: near}) + s]
                send(late, src, R2B.at[(i, near) + s], dev)
        return early, late

    def scatter3(parts, where):
        if parts is KV:
            return where[0]
        early, late = where
        arrived(early)
        for part, col, n in parts:
            axis, rest, left = others(part, 1)
            s = (slice(None), pl.ds(col, n))
            for i, k in enumerate((1, 3)):
                half = pl.ds(2 * i, 2)
                own = S1[place(left, {axis: (me[axis] + k) % 4, rest[0]: half}) + s]
                at = (i, slice(None)) + s
                R2A[at] = (own.astype(F32) + R2A[at].astype(F32)).astype(BF16)
                send(late, R2A.at[at], R2B.at[(i, half) + s], device(shifted(axis, k), c))
        return late

    def scatter4(parts, where):
        arrived(where)
        where = stage(R3.at[:, :, columns(parts)])
        came = [R2C.at[k] for k in range(3)] if parts is KV else [R2B.at[k] for k in range(2)]
        for part, col, n in parts:
            axis, rest, left = others(part, 1)
            s = (slice(None), pl.ds(col, n))
            t = S1[place(left, {axis: me[axis]}) + s].astype(F32)
            for ref in came:
                t = t + ref[(slice(None),) + s].astype(F32)
            S2[(slice(None),) + s] = t.astype(BF16)
            axis, rest, left = others(part, 2)
            for k in (1, 2, 3):
                to = shifted(axis, k)
                send(where, S2.at[(to[axis],) + s], R3.at[(k - 1,) + s], device(to, c))
        return where

    def scatter5(parts, where, i):
        arrived(where)
        for part, col, n in parts:
            axis, rest, left = others(part, 2)
            s = (slice(None), pl.ds(col, n))
            t = S2[(me[axis],) + s].astype(F32)
            for k in range(3):
                t = t + R3[(k,) + s].astype(F32)
            KEEP[:, s[1]] = t[0:8, :] * c0 + t[8:16, :] * c1
            FSEND[:, s[1]] = t[0:8, :] * c1 + t[8:16, :] * c0
        s = columns(parts)
        copy = remote(FSEND.at[:, s], FRECV.at[:, s], ex_s.at[7 + i], ex_r.at[7 + i], sibling)
        copy.start()
        return copy

    def halves(col, n):
        keep = KEEP[:, col : col + n]
        got = FRECV[:, col : col + n]
        return keep * c0 + got * c1, keep * c1 + got * c0

    def finish(copy, *cols):
        copy.wait_recv()
        puts = []
        for col in cols:
            if col in (CQ, CK):
                i = (CQ, CK).index(col)
                lo, hi = halves(col, 512)
                OUT8[i, :, :512] = lo
                OUT8[i, :, 512:] = hi
                puts.append((OUT8.at[i], (gq_ref, gk_ref)[i]))
            elif col == VTILE:
                lo, hi = halves(col, 128)
                OUTVEC[...] = jnp.concatenate([lo + hi, jnp.zeros((120, 128), F32)], axis=0).T[96:104, :]
                puts.append((OUTVEC, vec_ref))
            else:
                i = (CV, CG, CO, CMG, CMU, CMD).index(col)
                lo, hi = halves(col, WIDE)
                moved = pltpu.roll(jnp.concatenate([hi, jnp.zeros((8, 128), F32)], axis=1), 96, 1)
                first96 = lax.broadcasted_iota(jnp.int32, (8, 128), 1) < 96
                OUTW[i, :, 0:768] = lo[:, 0:768]
                OUTW[i, :, 768:896] = jnp.where(first96, lo[:, 768:896], moved[:, 0:128])
                OUTW[i, :, 896:1728] = moved[:, 128:960]
                puts.append((OUTW.at[i], (gv_ref, gg_ref, go_ref, gmg_ref, gmu_ref, gmd_ref)[i]))
        for src, dst in puts:
            out = pltpu.make_async_copy(src, dst, loc.at[14 + len(written)])
            out.start()
            written.append(out)
        return copy

    written = []

    def emit_hidden(at, w, r):
        GGL[:, at : at + w] = (r * ACT[:, at : at + w]).astype(BF16)
        GUL[:, at : at + w] = (r * BCT[:, at : at + w]).astype(BF16)

    def gmd():
        transpose(G, TT)
        grad(TT, HID, CMD)

    def gh():
        fwd(G, CMD, WIDE, emit_hidden)

    def second_body(i):
        r = mm_nt(GGL[...], wrows(i, CMG, WIDE)) + mm_nt(GUL[...], wrows(i, CMU, WIDE))
        s = pl.ds(i * 256, 256)
        GM[:, s] = r
        SB[:, s] = r.astype(BF16)
        remote(SB.at[:, s], RB2.at[:, s], ex_s.at[5], ex_r.at[5], sibling).start()

    def gs():
        e_mid.wait_send()
        each(4, second_body)

    e_sec = remote(SB, RB2, ex_s.at[5], ex_r.at[5], sibling)

    def gmg():
        transpose(SEC, TT)
        grad(TT, GGL, CMG)

    def gmu():
        transpose(SEC, TT)
        grad(TT, GUL, CMU)

    def norm_back(gs, v, gain, at, which):
        rstd = STAT[which + 1, at, 0:1]
        xh = (v - STAT[which, at, 0:1]) * rstd
        gx = gs * gain
        m0 = jnp.mean(gx, axis=-1, keepdims=True)
        m1 = jnp.mean(gx * xh, axis=-1, keepdims=True)
        return rstd * (gx - m0 - xh * m1), jnp.sum(gs * xh, axis=0, keepdims=True), jnp.sum(gs, axis=0, keepdims=True)

    def ln2b():
        gain2 = vector(2)

        def ln2_back(i):
            gs = GM[rows(i), :] + RB2[rows(i), :].astype(F32)
            part, ggain, gbias = norm_back(gs, MID[rows(i), :], gain2, rows(i), 2)
            gm = G[rows(i), :].astype(F32) + part
            GM[rows(i), :] = gm
            GML[rows(i), :] = gm.astype(BF16)
            mine = (i // 2 == c).astype(F32)
            VA[2:3, :] += ggain * mine
            VA[3:4, :] += gbias * mine

        e_sec.wait_recv()
        loop(4, ln2_back)

    def gout():
        transpose(GML, TT)
        grad(TT, GATED, CO)

    def emit_gated(at, w, r):
        ACT[:, at : at + w] = r

    def gated():
        fwd(GML, CO, WIDE, emit_gated)

    def group_back(i):
        gr = ACT[rows(i), :]
        z = GATE[rows(i), :]
        sg = jax.nn.sigmoid(z)
        grp = GRP[rows(i), :]
        GGP[rows(i), :] = (gr * (sg * (1.0 + z * (1.0 - sg))) * grp).astype(BF16)
        gg = gr * (z * sg)
        gmx = RSTD[rows(i), :] * (gg - heads_mean(gg) - grp * heads_mean(gg * grp))
        GMX[rows(i), :] = jnp.where(real, gmx, 0.0).astype(BF16)

    def groupb():
        loop(4, group_back)

    def gc():
        transpose(GMX, VT)
        u_sent()
        for hh in range(2):
            r = mm(VT[VH * hh : VH * (hh + 1), :], QS[:, 256 * hh : 256 * (hh + 1)])
            UT[VH * hh : VH * (hh + 1), :] = r.astype(BF16)

    def gg():
        grad(NORMT, GGP, CG)

    def gq():
        grad(NORMT, GQ, CQ)

    wide = lax.broadcasted_iota(jnp.int32, (256, 512), 1)
    windows = (slice(0, 512), slice(384, 896))

    def window(ref, hh):
        a = ref[:, windows[hh]]
        keep = wide < VH if hh == 0 else wide >= VH - 384
        return jnp.where(keep, a, jnp.zeros_like(a))

    def spots(hh, offset, sign):
        spot = lax.broadcasted_iota(jnp.int32, (256, 128), 0).astype(F32)
        return jnp.exp((spot * sign + offset) * lg[hh])

    def unrotated(dst, src, hh, cross, offset, sign, scale):
        sc = spots(hh, offset, sign)
        co, si = COS[...], SIN[...]
        a, b = slice(256 * hh, 256 * hh + 128), slice(256 * hh + 128, 256 * hh + 256)
        u = (src[:, a] + cross[:, :128] * sc) * scale
        z = (src[:, b] + cross[:, 128:] * sc) * scale
        dst[:, a] = (u * co + z * si).astype(BF16)
        dst[:, b] = (z * co - u * si).astype(BF16)

    def intra():
        gvi = []
        for hh in range(2):
            h = slice(256 * hh, 256 * (hh + 1))
            gm = window(GMX, hh)
            vw = V[:, windows[hh]]
            graw = (mm_nt(gm, vw) * MASK[hh]).astype(BF16)
            ACT[:, h] = mm(graw, K[:, h])
            BCT[:, h] = mm(graw.T, Q[:, h])
            gvi.append(mm(WT[hh].T, gm))
            unrotated(GQ, ACT, hh, mm(gm, CT[windows[hh], :]), 1.0, 1.0, 1.0)
        join(MIX, gvi[0], gvi[1])

    def down_body(i):
        r = mm_nt(HID[...], wrows(i, CMD, WIDE))
        s = pl.ds(i * 256, 256)
        OWN1[:, s] = r[0:128] * c0 + r[128:256] * c1
        SBO[:, s] = (r[0:128] * c1 + r[128:256] * c0).astype(BF16)

    e_out = remote(SBO, RBO, ex_s.at[4], ex_r.at[4], sibling)
    put_out = pltpu.make_async_copy(OUTV.at[0], out_ref, loc.at[12])
    put_gin = pltpu.make_async_copy(OUTV.at[1], gin_ref, loc.at[13])

    def down():
        each(4, down_body)
        e_out.start()

    def normed_first(i):
        r = mm_nt(GQ[...], wrows(i, CQ, 512)) + mm_nt(GGP[...], wrows(i, CG, WIDE))
        MID[:, pl.ds(i * 256, 256)] = r

    def pn1():
        e_out.wait_recv()
        OUTV[0] = (MID[rows_own, :] + OWN1[...] + RBO[...].astype(F32)).astype(BF16)
        put_out.start()
        each(4, normed_first)

    def kvb():
        gvs = []
        for hh in range(2):
            h = slice(256 * hh, 256 * (hh + 1))
            unrotated(GK, BCT, hh, mm(window(V, hh), GUT[windows[hh], :]), 255.0, -1.0, 0.0625)
            gvs.append(mm_nt(KW[:, h], GUT[windows[hh], :]))
        join(ACT, gvs[0], gvs[1])
        GV[...] = (MIX[...] + ACT[...]).astype(BF16)

    def gk():
        grad(NORMT, GK, CK)

    def gv():
        grad(NORMT, GV, CV)

    def normed_body(i):
        s = pl.ds(i * 256, 256)
        r = MID[:, s] + mm_nt(GK[...], wrows(i, CK, 512)) + mm_nt(GV[...], wrows(i, CV, WIDE))
        OWN2[:, s] = r[0:128] * c0 + r[128:256] * c1
        SBO[:, s] = (r[0:128] * c1 + r[128:256] * c0).astype(BF16)
        remote(SBO.at[:, s], RB3.at[:, s], ex_s.at[6], ex_r.at[6], sibling).start()

    def pn2():
        e_out.wait_send()
        each(4, normed_body)

    e_norm = remote(SBO, RB3, ex_s.at[6], ex_r.at[6], sibling)

    def ln1b():
        gain1 = vector(0)

        def ln1_back(i):
            at = pl.ds(pl.multiple_of(c * 128 + i * 64, 64), 64)
            gs = OWN2[rows(i), :] + RB3[rows(i), :].astype(F32)
            part, ggain, gbias = norm_back(gs, X[at, :].astype(F32), gain1, at, 0)
            OUTV[1, rows(i), :] = (GM[at, :] + part).astype(BF16)
            VA[0:1, :] += ggain
            VA[1:2, :] += gbias

        e_norm.wait_recv()
        loop(2, ln1_back)
        put_gin.start()
        vectors = jnp.concatenate([jnp.zeros((96, 1024), F32), VA[...], jnp.zeros((24, 1024), F32)], axis=0).T
        tile = slice(VTILE, VTILE + 128)
        Gd[:, :, :, :, tile] = (
            Gd[:, :, :, :, tile].astype(F32) + vectors.reshape(4, 4, 4, 16, 128)
        ).astype(BF16)

    w1(0)
    w1(2)
    w1(1)
    w1(4)
    w1(3)
    w2(2)
    w2(1)
    w3(0)
    w3(1)
    w4(0)
    w2(3)
    w3(2)
    w2(4)
    w4(1)
    w5(0)
    ln1()
    kvu()
    u_middle, u_finish, u_sent = states(UT, 0, False)
    w3(3)
    w3(4)
    u_middle(0, 1, 2, 3)
    w5(1)
    w4(2)
    w4(3)
    transpose(NORM, NORMT)
    gate()
    qi()
    u_finish(CT)
    cross()
    gn()
    w5(2)
    out()
    w4(4)
    ln2()
    w5(3)
    mlp()
    gelu()
    gmd()
    w5(4)
    r_down = scatter0(DOWN)
    gh()
    gs()
    gmg()
    gmu()
    r_mlp = scatter0(MLP)
    ln2b()
    r_down = scatter1(DOWN, r_down)
    gout()
    gated()
    groupb()
    gc()
    c_middle, c_finish, c_sent = states(UT, 8, True)
    r_out = scatter0(OUT)
    intra()
    down()
    gq()
    gg()
    r_qg = scatter0(QG)
    c_middle(0, 1)
    c_middle(2, 3)
    r_mlp = scatter1(MLP, r_mlp)
    r_out = scatter1(OUT, r_out)
    r_qg = scatter1(QG, r_qg)
    c_finish(GUT)
    kvb()
    gv()
    gk()
    r_kv = scatter0(KV_EARLY, stage(RB1.at[:, :, :, :, columns(KV)]))
    r_mlp = scatter2(MLP, r_mlp)
    pn1()
    pn2()
    ln1b()
    r_vec = scatter0(KV_LATE, r_kv[1])
    r_kv = scatter1(KV_EARLY, r_kv)
    scatter1(KV_LATE, r_vec)
    r_down = scatter2(DOWN, r_down)
    r_qg = scatter2(QG, r_qg)
    r_out = scatter2(OUT, r_out)
    r_mlp = scatter3(MLP, r_mlp)
    r_down = scatter3(DOWN, r_down)
    r_kv = scatter2(KV, r_kv)
    r_out = scatter3(OUT, r_out)
    r_qg = scatter3(QG, r_qg)
    r_mlp = scatter4(MLP, r_mlp)
    r_down = scatter4(DOWN, r_down)
    r_kv = scatter3(KV, r_kv)
    r_kv = scatter4(KV, r_kv)
    r_out = scatter4(OUT, r_out)
    r_qg = scatter4(QG, r_qg)
    f_mlp = scatter5(MLP, r_mlp, 1)
    f_out = scatter5(OUT, r_out, 2)
    f_down = scatter5(DOWN, r_down, 0)
    f_kv = scatter5(KV, r_kv, 4)
    f_qg = scatter5(QG, r_qg, 3)
    f_mlp = finish(f_mlp, CMG, CMU)
    f_out = finish(f_out, CO)
    f_down = finish(f_down, CMD)
    f_kv = finish(f_kv, CK, CV, VTILE)
    f_qg = finish(f_qg, CQ, CG)
    c_sent()
    put_out.wait()
    put_gin.wait()
    for where in pending:
        remote(where[2], where[2], where[0], where[1], sibling).wait_send()
    for copy in (e_first, e_rest, e_x, e_g, e_sec, e_norm):
        copy.wait_send()
    for copy in (f_down, f_mlp, f_out, f_qg, f_kv):
        copy.wait_send()
    for out in written:
        out.wait()


def hand_over(*refs):
    vec, results, smalls, outs, rows, held = refs[0], refs[1:11], refs[11:15], refs[15:25], refs[25], refs[26:36]
    sems = refs[36]
    fetch = [pltpu.make_async_copy(a, b, sems.at[i]) for i, (a, b) in enumerate(zip(results, held))]
    write = [pltpu.make_async_copy(a, b, sems.at[10 + i]) for i, (a, b) in enumerate(zip(held, outs))]
    last = pltpu.make_async_copy(vec, rows, sems.at[20])
    for copy in fetch:
        copy.start()
    last.start()
    for a, b in zip(fetch, write):
        a.wait()
        b.start()
    last.wait()
    for i, ref in enumerate(smalls):
        ref[...] = rows[i : i + 1, 0:8]
    for copy in write:
        copy.wait()


def scratch():
    def b(*shape):
        return pltpu.VMEM(shape, BF16)

    def f(*shape):
        return pltpu.VMEM(shape, F32)

    def sem(n):
        return pltpu.SemaphoreType.DMA((n,))

    return [
        b(4, 4, 4, 16, TOTAL), b(4, 4, 4, 16, TOTAL), b(2, 2, 4, 16, TOTAL), b(2, 4, 4, 16, TOTAL),
        b(2, 2, 16, TOTAL), b(2, 4, 16, TOTAL), b(3, 4, 16, CQ), b(3, 16, TOTAL),
        b(256, 1024), b(256, 1024), f(8, 1792), b(2, 8, 1024), b(6, 8, 1728), f(8, 128), f(2, 8, 1024), f(6, 8, 1728), f(8, 128),
        b(2, 128, 1024), b(16, TOTAL), b(2, 16, TOTAL), f(8, 1024), f(8, 1024),
        f(256, 128), f(256, 128), f(4, 256, 128),
        b(256, 1024), b(1024, 256), b(1024, 256), b(256, 512), b(256, 512), b(256, 512), b(256, 512),
        b(256, WIDE), b(256, WIDE), f(256, WIDE), b(2, 256, 256), f(2, 256, 256), f(256, WIDE), f(256, WIDE),
        b(REAL, 256), b(REAL, 256), b(3, REAL, 256), b(WIDE, 256), b(WIDE, 256),
        b(256, WIDE), f(256, 1024), b(256, 1024), b(256, 1024), b(128, 1024), b(128, 1024), f(128, 1024),
        b(256, 1024), b(128, 1024), f(128, 1024),
        b(256, 1024), f(256, WIDE), f(256, WIDE), b(256, WIDE), b(256, WIDE), b(256, WIDE),
        f(256, 1024), b(256, WIDE), b(256, 512), b(256, 512), b(256, WIDE),
        f(8, TOTAL), f(8, TOTAL), f(8, TOTAL),
        sem(52), sem(52), sem(16), sem(16), sem(13), sem(13), sem(24),
    ]


def per_device(
    inputs, cotangent, ln1_gain, ln1_bias, w_query, w_key, w_value, w_gate, w_out,
    ln2_gain, ln2_bias, w_mlp_gate, w_mlp_up, w_mlp_down,
):
    cosine, sine = tables()
    anywhere = pl.BlockSpec(memory_space=pl.ANY)
    here = pl.BlockSpec(memory_space=pltpu.VMEM)
    tokens = jax.ShapeDtypeStruct((128, 1024), BF16)
    square = jax.ShapeDtypeStruct((8, 1024), F32)
    wide = jax.ShapeDtypeStruct((8, 1728), F32)
    small = jax.ShapeDtypeStruct((1, 8), F32)
    results = [tokens] * 2 + [square] * 2 + [wide] * 6
    vectors = (ln1_gain, ln1_bias, ln2_gain, ln2_bias)
    out, gin, vec, *grads = pl.pallas_call(
        kernel,
        out_shape=results[:2] + [jax.ShapeDtypeStruct((8, 128), F32)] + results[2:],
        in_specs=[here] * 4 + [anywhere] * 12,
        out_specs=[anywhere] * 11,
        scratch_shapes=scratch(),
        compiler_params=pltpu.CompilerParams(
            collective_id=0, has_side_effects=True, vmem_limit_bytes=64 << 20
        ),
        name="block",
    )(
        *(v.reshape(1, 8) for v in vectors), inputs[0], cotangent[0], w_query, w_key, w_value, w_gate, w_out.T,
        w_mlp_gate, w_mlp_up, w_mlp_down.T, jnp.asarray(cosine), jnp.asarray(sine),
    )
    *smalls, out, gin, gq, gk, gv, gg, go, gmg, gmu, gmd = pl.pallas_call(
        hand_over,
        out_shape=[small] * 4 + results,
        in_specs=[anywhere] * 11,
        out_specs=[here] * 4 + [anywhere] * 10,
        scratch_shapes=[pltpu.VMEM((8, 128), F32)]
        + [pltpu.VMEM(r.shape, r.dtype) for r in results]
        + [pltpu.SemaphoreType.DMA((21,))],
        compiler_params=pltpu.CompilerParams(vmem_limit_bytes=64 << 20),
        name="hand_over",
    )(vec, out, gin, *grads)
    a, b, c, d = (v.reshape(8) for v in smalls)
    return out[None], gin[None], a, b, gq, gk, gv, gg, go.T, c, d, gmg, gmu, gmd.T


def solution(mesh):
    both = ("dp", "seq")
    row, col, vec, tokens = P(both, None), P(None, both), P(both), P("dp", "seq", None)
    return jax.shard_map(
        per_device,
        mesh=mesh,
        in_specs=(tokens, tokens, vec, vec, row, row, row, row, col, vec, vec, row, row, col),
        out_specs=(tokens, tokens, vec, vec, row, row, row, row, col, vec, vec, row, row, col),
        check_vma=False,
    )
```

time: 145 us -> 131 us (0.903)
  local copies, waits for them, and re-layouts: 7.11 us -> 0 us
  Pallas kernels: 137 us -> 130 us
    pallas_call x1 -> x2, Pallas kernels: 137 us -> 130 us  [the longest x1 128 us: per_device(): pl.pallas_call(kernel, out_shape=results[:2] + [jax.ShapeDtypeStruct((8,...]
    slice x2 -> x0, local copies, waits for them, and re-layouts: 2.97 us -> none  [the longest x1 1.57 us: per_device(): vec = [pack[:, OVEC + 96 + i] for i in range(4)]]
    unnamed x14 -> x0, local copies, waits for them, and re-layouts: 2.42 us -> none
    transpose x1 -> x0, local copies, waits for them, and re-layouts: 1.72 us -> none  [per_device(): return (out[None], gin[None], vec[0], vec[1], pack[:, OQ:OQ + 1024], pack...]
where the time goes in v1:
time: 131 us
  Pallas kernels  130 us (99%)
    pallas_call x1, Pallas kernels, per_device(): pl.pallas_call(kernel, out_shape=results[:2] + [jax.ShapeDtypeStruct((8,...  128 us

profile of v1, /device:TPU:1, one launch (start us, length us, event | category | flops | bytes accessed | tf_op | source)
XLA Modules:
  0.0 131.2 jit_solution(1883610592919329744)
XLA Ops:
  0.7 127.7 %block.1 = (bf16[128,1024]{1,0:T(8,128)(2,1)}, bf16[128,1024]{1,0:T(8,128)(2,1)}, f32[8,128]{1,0:T(8,128)}, f32[8,1024]{1,0:T(8,128)}, f32[8,1024]{1,0:T(8,128)}...) custom-call(bf16[1,8]{1,0:T(2,128)(2,1)} %bitcast.20, ...), custom_call_target="tpu_custom_call" | custom-call | tf_op jit(solution)/shard_map/block/pallas_call | solution.py:1067
  128.4 2.6 %hand_over.1 = (f32[1,8]{1,0:T(1,128)}, f32[1,8]{1,0:T(1,128)}, f32[1,8]{1,0:T(1,128)}, f32[1,8]{1,0:T(1,128)}, bf16[128,1024]{1,0:T(8,128)(2,1)}, /*index=5*/bf...) custom-call(f32[8,128]{1,0:T(8,128)} %get-tuple-element.39.refs_0_, ...), custom_call_target="tpu_custom_call" | custom-call | tf_op jit(solution)/shard_map/hand_over/pallas_call | solution.py:1081

commit v2 on v1

--- a/solution.py
+++ b/solution.py
@@ -29,11 +29,11 @@
 
 
 GATHERS = (
-    cut(CK, 4, 3, 4), cut(CQ, 4, 4, 3), cut(CO, 2, 2, 3), cut(CMG, 6, 2, 6), cut(CMD, 3, 2, 2),
+    cut(CK, 4, 4, 3), cut(CQ, 5, 1, 5), cut(CO, 2, 2, 3), cut(CMG, 6, 4, 4), cut(CMD, 2, 2, 3),
 )
 KV = cut(CK, 4, 4, 3)
 KV_EARLY, KV_LATE = cut(CK, 4, 4, 2), ((2, VTILE, 128),)
-QG, OUT, MLP, DOWN = cut(CQ, 5, 3, 3), cut(CO, 1, 2, 4), cut(CMG, 6, 2, 6), cut(CMD, 3, 3, 1)
+QG, OUT, MLP, DOWN = cut(CQ, 4, 2, 5), cut(CO, 2, 2, 3), cut(CMG, 7, 3, 4), cut(CMD, 1, 3, 3)
 FORWARD_GATHERS = (1, 2, 3, 4,)
 PIECES = ((slice(0, 224), 0), (slice(224, 432), 0), (slice(432, 656), 1), (slice(656, 864), 1))
 ORDERS = (("x", "y", "z"), ("y", "z", "x"), ("z", "x", "y"))
@@ -110,13 +110,11 @@
     rows_sib = pl.ds(pl.multiple_of((1 - c) * 128, 128), 128)
     fetch = [
         pltpu.make_async_copy(src, dst, loc.at[i])
-        for i, (src, dst) in enumerate(
-            (
-                (wq_in, IN8.at[0]), (wk_in, IN8.at[1]), (wv_in, INW.at[0]), (wg_in, INW.at[1]),
-                (wo_in, INW.at[2]), (wmg_in, INW.at[3]), (wmu_in, INW.at[4]), (wmd_in, INW.at[5]),
-                (x_in, X.at[rows_own, :]), (g_in, G.at[rows_own, :]),
-                (cos_in.at[me["x"]], COS), (sin_in.at[me["x"]], SIN),
-            )
+        for src, dst, i in (
+            (wq_in, IN8.at[0], 0), (wk_in, IN8.at[1], 0), (wv_in, INW.at[0], 1), (wg_in, INW.at[1], 1),
+            (wo_in, INW.at[2], 1), (wmg_in, INW.at[3], 1), (wmu_in, INW.at[4], 1), (wmd_in, INW.at[5], 1),
+            (x_in, X.at[rows_own, :], 2), (g_in, G.at[rows_own, :], 3),
+            (cos_in.at[me["x"]], COS, 4), (sin_in.at[me["x"]], SIN, 5),
         )
     ]
     for copy in fetch:
@@ -173,8 +171,8 @@
     INV[...] = jnp.zeros_like(INV)
     for i, ref in enumerate((gain1_in, bias1_in, gain2_in, bias2_in)):
         INV[i : i + 1, 0:8] = ref[...].astype(F32)
-    for copy in fetch[:8]:
-        copy.wait()
+    pltpu.make_async_copy(IN8, IN8, loc.at[0]).wait()
+    pltpu.make_async_copy(INW, INW, loc.at[1]).wait()
     pack_square(1, CK)
     pack_wide(0, CV)
     pl.semaphore_wait(barrier, 10)
@@ -182,7 +180,7 @@
     pack_square(0, CQ)
     for i, col in enumerate((CG, CO, CMG, CMU, CMD)):
         pack_wide(i + 1, col)
-    e_rest = exchange(CQ, TOTAL, 12)
+    e_rest = exchange(CQ, TOTAL, 8)
     fetch[8].wait()
     e_x = remote(X.at[rows_own, :], X.at[rows_own, :], ex_s.at[1], ex_r.at[1], sibling)
     e_x.start()
@@ -190,12 +188,11 @@
     e_g = remote(G.at[rows_own, :], G.at[rows_own, :], ex_s.at[2], ex_r.at[2], sibling)
     e_g.start()
 
-    pending = []
     count = [0]
 
-    def stage(total):
+    def stage(kind, total):
         count[0] += 1
-        return way_s.at[count[0] - 1], way_r.at[count[0] - 1], total
+        return way_s.at[kind], way_r.at[count[0] - 1], total
 
     def send(where, src, dst, dev):
         remote(src, dst, where[0], where[1], dev).start()
@@ -203,7 +200,6 @@
     def arrived(where):
         ss, rs, total = where
         remote(total, total, ss, rs, sibling).wait_recv()
-        pending.append(where)
 
     def columns(parts):
         return pl.ds(parts[0][1], sum(n for _, _, n in parts))
@@ -212,9 +208,9 @@
         s = columns(GATHERS[group])
         halves = phase == 2 or (phase == 1 and group in FORWARD_GATHERS)
         if phase == 1:
-            where = stage(W.at[0, 0 : 1 if forward else 2 if halves else 3, :, :, s])
+            where = stage(3 if forward else 2 if halves else 1, W.at[0, 0 : 1 if forward else 2 if halves else 3, :, :, s])
         else:
-            where = stage(W.at[0, :, :, :, s] if forward else W.at[0:2, :, :, :, s])
+            where = stage(5, W.at[0, :, :, :, s]) if forward else stage(4, W.at[0:2, :, :, :, s])
         gather_parts(where, GATHERS[group], phase, halves, forward)
         return where
 
@@ -232,8 +228,26 @@
                 src = W.at[tuple(idx[a] for a in ZYX) + (slice(None), pl.ds(col, n))]
                 send(where, src, src, device(shifted(axis, k), c))
 
+    def early_third(g):
+        p4[g] = stage(4, W.at[0:2, :, :, :, columns(GATHERS[g])])
+        for part, col, n in GATHERS[g]:
+            a, b, axis = ORDERS[part]
+            idx = {a: slice(None), b: me[b], axis: me[axis]}
+            src = W.at[tuple(idx[q] for q in ZYX) + (slice(None), pl.ds(col, n))]
+            for k in (1, 3):
+                send(p4[g], src, src, device(shifted(axis, k), c))
+
+    def late_third(g):
+        for part, col, n in GATHERS[g]:
+            a, b, axis = ORDERS[part]
+            for j in (1, 2, 3):
+                idx = {a: slice(None), b: (me[b] + j) % 4, axis: me[axis]}
+                src = W.at[tuple(idx[q] for q in ZYX) + (slice(None), pl.ds(col, n))]
+                for k in (1, 3):
+                    send(p4[g], src, src, device(shifted(axis, k), c))
+
     def first_phase(groups, first, last):
-        where = stage(W.at[0, 0, 0:3, :, first:last])
+        where = stage(0, W.at[0, 0, 0:3, :, first:last])
         for g in groups:
             gather_parts(where, GATHERS[g], 0, False, False)
         return where
@@ -259,7 +273,7 @@
 
     def w3(g):
         arrived(p3[g] if g in FORWARD_GATHERS else p2[g])
-        p4[g] = gather(g, 2)
+        late_third(g)
 
     def w4(g):
         arrived(p4[g])
@@ -387,14 +401,14 @@
         for i, (at, hh) in enumerate(PIECES):
             t = base + i
             slot = 1 if back else 0
-            one = remote(src.at[at], STATES.at[slot, at], st_s.at[t], st_r.at[t], device(near, c))
+            one = remote(src.at[at], STATES.at[slot, at], st_s.at[base // 4], st_r.at[t], device(near, c))
             pl.when(sends)(one.start)
             steps.append(one)
 
         def second(i):
             at, hh = PIECES[i]
             t = base + 4 + i
-            two = remote(TOT.at[at], STATES.at[2, at], st_s.at[t], st_r.at[t], device(far, c))
+            two = remote(TOT.at[at], STATES.at[2, at], st_s.at[base // 4 + 1], st_r.at[t], device(far, c))
 
             def total():
                 steps[i].wait_recv()
@@ -433,9 +447,10 @@
                 pl.when(x == three)(triple)
 
         def sent():
-            for one, two in zip(steps, twos):
-                pl.when(sends)(one.wait_send)
-                pl.when(passes)(two.wait_send)
+            one = remote(src, src, st_s.at[base // 4], st_r.at[base], sibling)
+            two = remote(TOT, TOT, st_s.at[base // 4 + 1], st_r.at[base], sibling)
+            pl.when(sends)(one.wait_send)
+            pl.when(passes)(two.wait_send)
 
         twos = []
 
@@ -541,8 +556,8 @@
 
     def scatter0(parts, late=None):
         s = columns(parts)
-        early = stage(RA.at[:, :, :, :, s])
-        late = late or stage(RB1.at[:, :, :, :, s])
+        early = stage(6, RA.at[:, :, :, :, s])
+        late = late or stage(7, RB1.at[:, :, :, :, s])
         for where in (early, late):
             for part, col, n in parts:
                 axis, rest, left = others(part, 0)
@@ -581,9 +596,9 @@
         arrived(late)
         direct = parts is KV
         if direct:
-            early = stage(R2C.at[:, :, :, columns(parts)])
+            early = stage(8, R2C.at[:, :, :, columns(parts)])
         else:
-            early, late = stage(R2A.at[:, :, :, columns(parts)]), stage(R2B.at[:, :, :, columns(parts)])
+            early, late = stage(9, R2A.at[:, :, :, columns(parts)]), stage(10, R2B.at[:, :, :, columns(parts)])
         for part, col, n in parts:
             axis, rest, left = others(part, 0)
             s = (slice(None), pl.ds(col, n))
@@ -628,7 +643,7 @@
 
     def scatter4(parts, where):
         arrived(where)
-        where = stage(R3.at[:, :, columns(parts)])
+        where = stage(11, R3.at[:, :, columns(parts)])
         came = [R2C.at[k] for k in range(3)] if parts is KV else [R2B.at[k] for k in range(2)]
         for part, col, n in parts:
             axis, rest, left = others(part, 1)
@@ -654,7 +669,7 @@
             KEEP[:, s[1]] = t[0:8, :] * c0 + t[8:16, :] * c1
             FSEND[:, s[1]] = t[0:8, :] * c1 + t[8:16, :] * c0
         s = columns(parts)
-        copy = remote(FSEND.at[:, s], FRECV.at[:, s], ex_s.at[7 + i], ex_r.at[7 + i], sibling)
+        copy = remote(FSEND.at[:, s], FRECV.at[:, s], ex_s.at[7], ex_r.at[9 + i], sibling)
         copy.start()
         return copy
 
@@ -672,11 +687,11 @@
                 lo, hi = halves(col, 512)
                 OUT8[i, :, :512] = lo
                 OUT8[i, :, 512:] = hi
-                puts.append((OUT8.at[i], (gq_ref, gk_ref)[i]))
+                puts.append((OUT8.at[i], (gq_ref, gk_ref)[i], 8))
             elif col == VTILE:
                 lo, hi = halves(col, 128)
                 OUTVEC[...] = jnp.concatenate([lo + hi, jnp.zeros((120, 128), F32)], axis=0).T[96:104, :]
-                puts.append((OUTVEC, vec_ref))
+                puts.append((OUTVEC, vec_ref, 9))
             else:
                 i = (CV, CG, CO, CMG, CMU, CMD).index(col)
                 lo, hi = halves(col, WIDE)
@@ -685,14 +700,10 @@
                 OUTW[i, :, 0:768] = lo[:, 0:768]
                 OUTW[i, :, 768:896] = jnp.where(first96, lo[:, 768:896], moved[:, 0:128])
                 OUTW[i, :, 896:1728] = moved[:, 128:960]
-                puts.append((OUTW.at[i], (gv_ref, gg_ref, go_ref, gmg_ref, gmu_ref, gmd_ref)[i]))
-        for src, dst in puts:
-            out = pltpu.make_async_copy(src, dst, loc.at[14 + len(written)])
-            out.start()
-            written.append(out)
+                puts.append((OUTW.at[i], (gv_ref, gg_ref, go_ref, gmg_ref, gmu_ref, gmd_ref)[i], 10))
+        for src, dst, at in puts:
+            pltpu.make_async_copy(src, dst, loc.at[at]).start()
         return copy
-
-    written = []
 
     def emit_hidden(at, w, r):
         GGL[:, at : at + w] = (r * ACT[:, at : at + w]).astype(BF16)
@@ -827,8 +838,8 @@
         SBO[:, s] = (r[0:128] * c1 + r[128:256] * c0).astype(BF16)
 
     e_out = remote(SBO, RBO, ex_s.at[4], ex_r.at[4], sibling)
-    put_out = pltpu.make_async_copy(OUTV.at[0], out_ref, loc.at[12])
-    put_gin = pltpu.make_async_copy(OUTV.at[1], gin_ref, loc.at[13])
+    put_out = pltpu.make_async_copy(OUTV.at[0], out_ref, loc.at[6])
+    put_gin = pltpu.make_async_copy(OUTV.at[1], gin_ref, loc.at[7])
 
     def down():
         each(4, down_body)
@@ -894,51 +905,55 @@
 
     w1(0)
     w1(2)
+    early_third(0)
     w1(1)
-    w1(4)
     w1(3)
+    early_third(1)
+    w3(0)
+    early_third(3)
     w2(2)
     w2(1)
-    w3(0)
-    w3(1)
+    w1(4)
+    early_third(2)
     w4(0)
     w2(3)
+    w3(1)
     w3(2)
-    w2(4)
-    w4(1)
+    early_third(4)
     w5(0)
     ln1()
+    w2(4)
     kvu()
     u_middle, u_finish, u_sent = states(UT, 0, False)
     w3(3)
+    w4(1)
+    u_middle(0, 1, 2, 3)
+    w4(2)
     w3(4)
-    u_middle(0, 1, 2, 3)
     w5(1)
-    w4(2)
     w4(3)
-    transpose(NORM, NORMT)
     gate()
     qi()
     u_finish(CT)
+    w5(2)
     cross()
     gn()
-    w5(2)
     out()
+    transpose(NORM, NORMT)
     w4(4)
     ln2()
     w5(3)
     mlp()
     gelu()
     gmd()
+    r_down = scatter0(DOWN)
     w5(4)
-    r_down = scatter0(DOWN)
     gh()
     gs()
     gmg()
     gmu()
     r_mlp = scatter0(MLP)
     ln2b()
-    r_down = scatter1(DOWN, r_down)
     gout()
     gated()
     groupb()
@@ -946,62 +961,67 @@
     c_middle, c_finish, c_sent = states(UT, 8, True)
     r_out = scatter0(OUT)
     intra()
+    gg()
     down()
     gq()
-    gg()
     r_qg = scatter0(QG)
     c_middle(0, 1)
     c_middle(2, 3)
     r_mlp = scatter1(MLP, r_mlp)
-    r_out = scatter1(OUT, r_out)
+    r_down = scatter1(DOWN, r_down)
     r_qg = scatter1(QG, r_qg)
     c_finish(GUT)
     kvb()
+    gk()
     gv()
-    gk()
-    r_kv = scatter0(KV_EARLY, stage(RB1.at[:, :, :, :, columns(KV)]))
+    r_kv = scatter0(KV_EARLY, stage(7, RB1.at[:, :, :, :, columns(KV)]))
     r_mlp = scatter2(MLP, r_mlp)
     pn1()
     pn2()
+    r_out = scatter1(OUT, r_out)
+    r_down = scatter2(DOWN, r_down)
     ln1b()
     r_vec = scatter0(KV_LATE, r_kv[1])
     r_kv = scatter1(KV_EARLY, r_kv)
     scatter1(KV_LATE, r_vec)
-    r_down = scatter2(DOWN, r_down)
     r_qg = scatter2(QG, r_qg)
+    r_down = scatter3(DOWN, r_down)
+    r_mlp = scatter3(MLP, r_mlp)
     r_out = scatter2(OUT, r_out)
-    r_mlp = scatter3(MLP, r_mlp)
-    r_down = scatter3(DOWN, r_down)
+    r_qg = scatter3(QG, r_qg)
     r_kv = scatter2(KV, r_kv)
     r_out = scatter3(OUT, r_out)
-    r_qg = scatter3(QG, r_qg)
+    r_kv = scatter3(KV, r_kv)
+    r_down = scatter4(DOWN, r_down)
+    r_qg = scatter4(QG, r_qg)
     r_mlp = scatter4(MLP, r_mlp)
-    r_down = scatter4(DOWN, r_down)
-    r_kv = scatter3(KV, r_kv)
     r_kv = scatter4(KV, r_kv)
     r_out = scatter4(OUT, r_out)
-    r_qg = scatter4(QG, r_qg)
+    f_qg = scatter5(QG, r_qg, 3)
+    f_down = scatter5(DOWN, r_down, 0)
     f_mlp = scatter5(MLP, r_mlp, 1)
+    f_kv = scatter5(KV, r_kv, 4)
     f_out = scatter5(OUT, r_out, 2)
-    f_down = scatter5(DOWN, r_down, 0)
-    f_kv = scatter5(KV, r_kv, 4)
-    f_qg = scatter5(QG, r_qg, 3)
+    f_qg = finish(f_qg, CQ, CG)
+    f_down = finish(f_down, CMD)
     f_mlp = finish(f_mlp, CMG, CMU)
+    f_kv = finish(f_kv, CK, CV, VTILE)
     f_out = finish(f_out, CO)
-    f_down = finish(f_down, CMD)
-    f_kv = finish(f_kv, CK, CV, VTILE)
-    f_qg = finish(f_qg, CQ, CG)
     c_sent()
     put_out.wait()
     put_gin.wait()
-    for where in pending:
-        remote(where[2], where[2], where[0], where[1], sibling).wait_send()
+    most = pl.ds(CQ, TOTAL - CQ)
+    sent = (
+        W.at[0, 0, 0:3], W.at[0, 0:3, :, :, 0:CQ], W.at[0, 0:2, :, :, most], W.at[0, 0, :, :, most], W.at[0:2], W.at[0],
+        RA, RB1, R2C, R2A.at[:, :, :, most], R2B.at[:, :, :, most], R3,
+    )
+    for kind, total in enumerate(sent):
+        remote(total, total, way_s.at[kind], way_r.at[0], sibling).wait_send()
     for copy in (e_first, e_rest, e_x, e_g, e_sec, e_norm):
         copy.wait_send()
-    for copy in (f_down, f_mlp, f_out, f_qg, f_kv):
-        copy.wait_send()
-    for out in written:
-        out.wait()
+    remote(FSEND, FRECV, ex_s.at[7], ex_r.at[9], sibling).wait_send()
+    for ref, at in ((OUT8, 8), (OUTVEC, 9), (OUTW, 10)):
+        pltpu.make_async_copy(ref, ref, loc.at[at]).wait()
 
 
 def hand_over(*refs):
@@ -1047,7 +1067,7 @@
         b(256, 1024), f(256, WIDE), f(256, WIDE), b(256, WIDE), b(256, WIDE), b(256, WIDE),
         f(256, 1024), b(256, WIDE), b(256, 512), b(256, 512), b(256, WIDE),
         f(8, TOTAL), f(8, TOTAL), f(8, TOTAL),
-        sem(52), sem(52), sem(16), sem(16), sem(13), sem(13), sem(24),
+        sem(12), sem(46), sem(4), sem(16), sem(9), sem(14), sem(11),
     ]
 
 

time: 131 us -> 128 us (0.977)
  Pallas kernels: 130 us -> 127 us
    pallas_call x1, Pallas kernels: 128 us -> 125 us  [per_device(): pl.pallas_call(kernel, out_shape=results[:2] + [jax.ShapeDtypeStruct((8,...]
where the time goes in v2:
time: 128 us
  Pallas kernels  127 us (99%)
    pallas_call x1, Pallas kernels, per_device(): pl.pallas_call(kernel, out_shape=results[:2] + [jax.ShapeDtypeStruct((8,...  125 us
    pallas_call x1, Pallas kernels, per_device(): pl.pallas_call(hand_over, out_shape=[small] * 4 + results, in_specs=[anyw...  2.58 us

profile of v2, /device:TPU:1, one launch (start us, length us, event | category | flops | bytes accessed | tf_op | source)
XLA Modules:
  0.0 128.1 jit_solution(15081042700001981053)
XLA Ops:
  0.7 124.7 %block.1 = (bf16[128,1024]{1,0:T(8,128)(2,1)}, bf16[128,1024]{1,0:T(8,128)(2,1)}, f32[8,128]{1,0:T(8,128)}, f32[8,1024]{1,0:T(8,128)}, f32[8,1024]{1,0:T(8,128)}...) custom-call(bf16[1,8]{1,0:T(2,128)(2,1)} %bitcast.20, ...), custom_call_target="tpu_custom_call" | custom-call | tf_op jit(solution)/shard_map/block/pallas_call | solution.py:1087
  125.4 2.6 %hand_over.1 = (f32[1,8]{1,0:T(1,128)}, f32[1,8]{1,0:T(1,128)}, f32[1,8]{1,0:T(1,128)}, f32[1,8]{1,0:T(1,128)}, bf16[128,1024]{1,0:T(8,128)(2,1)}, /*index=5*/bf...) custom-call(f32[8,128]{1,0:T(8,128)} %get-tuple-element.39.refs_0_, ...), custom_call_target="tpu_custom_call" | custom-call | tf_op jit(solution)/shard_map/hand_over/pallas_call | solution.py:1101

commit v3 on v2

--- a/solution.py
+++ b/solution.py
@@ -29,11 +29,11 @@
 
 
 GATHERS = (
-    cut(CK, 4, 4, 3), cut(CQ, 5, 1, 5), cut(CO, 2, 2, 3), cut(CMG, 6, 4, 4), cut(CMD, 2, 2, 3),
+    cut(CK, 4, 4, 3), cut(CQ, 4, 2, 5), cut(CO, 3, 1, 3), cut(CMG, 5, 4, 5), cut(CMD, 3, 3, 1),
 )
 KV = cut(CK, 4, 4, 3)
 KV_EARLY, KV_LATE = cut(CK, 4, 4, 2), ((2, VTILE, 128),)
-QG, OUT, MLP, DOWN = cut(CQ, 4, 2, 5), cut(CO, 2, 2, 3), cut(CMG, 7, 3, 4), cut(CMD, 1, 3, 3)
+QG, OUT, MLP, DOWN = cut(CQ, 4, 1, 6), cut(CO, 3, 2, 2), cut(CMG, 6, 3, 5), cut(CMD, 2, 3, 2)
 FORWARD_GATHERS = (1, 2, 3, 4,)
 PIECES = ((slice(0, 224), 0), (slice(224, 432), 0), (slice(432, 656), 1), (slice(656, 864), 1))
 ORDERS = (("x", "y", "z"), ("y", "z", "x"), ("z", "x", "y"))
@@ -73,13 +73,13 @@
 
 def kernel(
     gain1_in, bias1_in, gain2_in, bias2_in, x_in, g_in, wq_in, wk_in, wv_in, wg_in, wo_in, wmg_in, wmu_in, wmd_in,
-    cos_in, sin_in, out_ref, gin_ref, vec_ref, gq_ref, gk_ref, gv_ref, gg_ref, go_ref, gmg_ref, gmu_ref, gmd_ref,
+    cos_in, sin_in, out_ref, gin_ref, OUTVEC, gq_ref, gk_ref, gv_ref, gg_ref, go_ref, gmg_ref, gmu_ref, gmd_ref,
     *scratch,
 ):
     (
-        W, Gd, RA, RB1, R2A, R2B, R2C, R3, X, G, WS, IN8, INW, INV, OUT8, OUTW, OUTVEC, OUTV, PSEND, PRECV, VEC, VA, COS, SIN, STAT,
-        NORM, NORMT, TT, Q, QS, K, KW, V, GGP, GATE, WT, MASK, MIX, GRP,
-        UT, TOT, STATES, CT, GUT, GATED, MID, SB, RB, SBO, RBO, OWN1, RB2, RB3, OWN2,
+        W, Gd, RA, RB1, R2A, R2B, R2C, R3, X, G, WS, IN8, INW, INV, PSEND, PRECV, VEC, VA, COS, SIN, STAT,
+        NORM, NORMT, TT, Q, QS, K, KW, V, GGP, GATE, WT, MIX, GRP,
+        UT, TOT, STATES, CT, GUT, GATED, MID, SB, RB, SBO, RBO, OWN1, RB2, RB3,
         SEC, ACT, BCT, HID, GGL, GUL, GM, GMX, GQ, GK, GV, FSEND, FRECV, KEEP,
         way_s, way_r, st_s, st_r, ex_s, ex_r, loc,
     ) = scratch
@@ -317,14 +317,12 @@
 
     lg = [log_gamma(0), log_gamma(1)]
 
-    def mask_body(i):
-        ii = lax.broadcasted_iota(jnp.int32, (64, 256), 0) + i * 64
-        jj = lax.broadcasted_iota(jnp.int32, (64, 256), 1)
-        d = (ii - jj).astype(F32)
-        for hh in range(2):
-            MASK[hh, rows(i), :] = jnp.where(d >= 0, jnp.exp(jnp.maximum(d, 0.0) * lg[hh]), 0.0)
-
-    loop(4, mask_body)
+    def mask(hh):
+        d = (
+            lax.broadcasted_iota(jnp.int32, (256, 256), 0) - lax.broadcasted_iota(jnp.int32, (256, 256), 1)
+        ).astype(F32)
+        return jnp.where(d >= 0, jnp.exp(jnp.maximum(d, 0.0) * lg[hh]), 0.0)
+
     VA[...] = jnp.zeros_like(VA)
     e_x.wait_recv()
     e_g.wait_recv()
@@ -469,7 +467,7 @@
         fwd(NORM, CQ, 512, rotated(Q, QS, 1.0, 1.0, 1.0))
         for hh in range(2):
             raw = mm_nt(Q[:, 256 * hh : 256 * (hh + 1)], K[:, 256 * hh : 256 * (hh + 1)])
-            WT[hh] = (raw * MASK[hh]).astype(BF16)
+            WT[hh] = (raw * mask(hh)).astype(BF16)
         join(MIX, mm(WT[0], V[:, 0:512]), mm(WT[1], V[:, 384:896]))
 
     def emit_gate(at, w, r):
@@ -680,29 +678,23 @@
 
     def finish(copy, *cols):
         copy.wait_recv()
-        puts = []
         for col in cols:
             if col in (CQ, CK):
-                i = (CQ, CK).index(col)
+                ref = (gq_ref, gk_ref)[(CQ, CK).index(col)]
                 lo, hi = halves(col, 512)
-                OUT8[i, :, :512] = lo
-                OUT8[i, :, 512:] = hi
-                puts.append((OUT8.at[i], (gq_ref, gk_ref)[i], 8))
+                ref[:, :512] = lo
+                ref[:, 512:] = hi
             elif col == VTILE:
                 lo, hi = halves(col, 128)
                 OUTVEC[...] = jnp.concatenate([lo + hi, jnp.zeros((120, 128), F32)], axis=0).T[96:104, :]
-                puts.append((OUTVEC, vec_ref, 9))
             else:
-                i = (CV, CG, CO, CMG, CMU, CMD).index(col)
+                ref = (gv_ref, gg_ref, go_ref, gmg_ref, gmu_ref, gmd_ref)[(CV, CG, CO, CMG, CMU, CMD).index(col)]
                 lo, hi = halves(col, WIDE)
                 moved = pltpu.roll(jnp.concatenate([hi, jnp.zeros((8, 128), F32)], axis=1), 96, 1)
                 first96 = lax.broadcasted_iota(jnp.int32, (8, 128), 1) < 96
-                OUTW[i, :, 0:768] = lo[:, 0:768]
-                OUTW[i, :, 768:896] = jnp.where(first96, lo[:, 768:896], moved[:, 0:128])
-                OUTW[i, :, 896:1728] = moved[:, 128:960]
-                puts.append((OUTW.at[i], (gv_ref, gg_ref, go_ref, gmg_ref, gmu_ref, gmd_ref)[i], 10))
-        for src, dst, at in puts:
-            pltpu.make_async_copy(src, dst, loc.at[at]).start()
+                ref[:, 0:768] = lo[:, 0:768]
+                ref[:, 768:896] = jnp.where(first96, lo[:, 768:896], moved[:, 0:128])
+                ref[:, 896:1728] = moved[:, 128:960]
         return copy
 
     def emit_hidden(at, w, r):
@@ -824,7 +816,7 @@
             h = slice(256 * hh, 256 * (hh + 1))
             gm = window(GMX, hh)
             vw = V[:, windows[hh]]
-            graw = (mm_nt(gm, vw) * MASK[hh]).astype(BF16)
+            graw = (mm_nt(gm, vw) * mask(hh)).astype(BF16)
             ACT[:, h] = mm(graw, K[:, h])
             BCT[:, h] = mm(graw.T, Q[:, h])
             gvi.append(mm(WT[hh].T, gm))
@@ -838,9 +830,6 @@
         SBO[:, s] = (r[0:128] * c1 + r[128:256] * c0).astype(BF16)
 
     e_out = remote(SBO, RBO, ex_s.at[4], ex_r.at[4], sibling)
-    put_out = pltpu.make_async_copy(OUTV.at[0], out_ref, loc.at[6])
-    put_gin = pltpu.make_async_copy(OUTV.at[1], gin_ref, loc.at[7])
-
     def down():
         each(4, down_body)
         e_out.start()
@@ -851,8 +840,7 @@
 
     def pn1():
         e_out.wait_recv()
-        OUTV[0] = (MID[rows_own, :] + OWN1[...] + RBO[...].astype(F32)).astype(BF16)
-        put_out.start()
+        out_ref[...] = (MID[rows_own, :] + OWN1[...] + RBO[...].astype(F32)).astype(BF16)
         each(4, normed_first)
 
     def kvb():
@@ -873,7 +861,7 @@
     def normed_body(i):
         s = pl.ds(i * 256, 256)
         r = MID[:, s] + mm_nt(GK[...], wrows(i, CK, 512)) + mm_nt(GV[...], wrows(i, CV, WIDE))
-        OWN2[:, s] = r[0:128] * c0 + r[128:256] * c1
+        OWN1[:, s] = r[0:128] * c0 + r[128:256] * c1
         SBO[:, s] = (r[0:128] * c1 + r[128:256] * c0).astype(BF16)
         remote(SBO.at[:, s], RB3.at[:, s], ex_s.at[6], ex_r.at[6], sibling).start()
 
@@ -888,15 +876,14 @@
 
         def ln1_back(i):
             at = pl.ds(pl.multiple_of(c * 128 + i * 64, 64), 64)
-            gs = OWN2[rows(i), :] + RB3[rows(i), :].astype(F32)
+            gs = OWN1[rows(i), :] + RB3[rows(i), :].astype(F32)
             part, ggain, gbias = norm_back(gs, X[at, :].astype(F32), gain1, at, 0)
-            OUTV[1, rows(i), :] = (GM[at, :] + part).astype(BF16)
+            gin_ref[rows(i), :] = (GM[at, :] + part).astype(BF16)
             VA[0:1, :] += ggain
             VA[1:2, :] += gbias
 
         e_norm.wait_recv()
         loop(2, ln1_back)
-        put_gin.start()
         vectors = jnp.concatenate([jnp.zeros((96, 1024), F32), VA[...], jnp.zeros((24, 1024), F32)], axis=0).T
         tile = slice(VTILE, VTILE + 128)
         Gd[:, :, :, :, tile] = (
@@ -904,25 +891,25 @@
         ).astype(BF16)
 
     w1(0)
+    w1(1)
+    w1(3)
     w1(2)
     early_third(0)
-    w1(1)
-    w1(3)
+    w3(0)
+    w2(1)
+    w2(2)
+    w1(4)
+    early_third(3)
+    w2(3)
+    w4(0)
     early_third(1)
-    w3(0)
-    early_third(3)
-    w2(2)
-    w2(1)
-    w1(4)
-    early_third(2)
-    w4(0)
-    w2(3)
+    early_third(4)
     w3(1)
-    w3(2)
-    early_third(4)
     w5(0)
     ln1()
     w2(4)
+    early_third(2)
+    w3(2)
     kvu()
     u_middle, u_finish, u_sent = states(UT, 0, False)
     w3(3)
@@ -930,16 +917,16 @@
     u_middle(0, 1, 2, 3)
     w4(2)
     w3(4)
+    transpose(NORM, NORMT)
+    w4(3)
+    u_finish(CT)
     w5(1)
-    w4(3)
     gate()
     qi()
-    u_finish(CT)
     w5(2)
     cross()
     gn()
     out()
-    transpose(NORM, NORMT)
     w4(4)
     ln2()
     w5(3)
@@ -949,67 +936,65 @@
     r_down = scatter0(DOWN)
     w5(4)
     gh()
+    gmu()
+    gmg()
+    r_mlp = scatter0(MLP)
     gs()
-    gmg()
-    gmu()
-    r_mlp = scatter0(MLP)
+    down()
     ln2b()
-    gout()
     gated()
     groupb()
     gc()
+    gout()
     c_middle, c_finish, c_sent = states(UT, 8, True)
     r_out = scatter0(OUT)
+    gg()
+    r_down = scatter1(DOWN, r_down)
     intra()
-    gg()
-    down()
     gq()
+    pn1()
     r_qg = scatter0(QG)
     c_middle(0, 1)
     c_middle(2, 3)
     r_mlp = scatter1(MLP, r_mlp)
-    r_down = scatter1(DOWN, r_down)
+    r_out = scatter1(OUT, r_out)
     r_qg = scatter1(QG, r_qg)
     c_finish(GUT)
     kvb()
+    gv()
     gk()
-    gv()
     r_kv = scatter0(KV_EARLY, stage(7, RB1.at[:, :, :, :, columns(KV)]))
+    pn2()
     r_mlp = scatter2(MLP, r_mlp)
-    pn1()
-    pn2()
-    r_out = scatter1(OUT, r_out)
-    r_down = scatter2(DOWN, r_down)
     ln1b()
     r_vec = scatter0(KV_LATE, r_kv[1])
     r_kv = scatter1(KV_EARLY, r_kv)
     scatter1(KV_LATE, r_vec)
     r_qg = scatter2(QG, r_qg)
-    r_down = scatter3(DOWN, r_down)
+    r_out = scatter2(OUT, r_out)
+    r_down = scatter2(DOWN, r_down)
     r_mlp = scatter3(MLP, r_mlp)
-    r_out = scatter2(OUT, r_out)
     r_qg = scatter3(QG, r_qg)
     r_kv = scatter2(KV, r_kv)
+    r_kv = scatter3(KV, r_kv)
+    r_down = scatter3(DOWN, r_down)
     r_out = scatter3(OUT, r_out)
-    r_kv = scatter3(KV, r_kv)
-    r_down = scatter4(DOWN, r_down)
     r_qg = scatter4(QG, r_qg)
     r_mlp = scatter4(MLP, r_mlp)
     r_kv = scatter4(KV, r_kv)
+    r_down = scatter4(DOWN, r_down)
     r_out = scatter4(OUT, r_out)
     f_qg = scatter5(QG, r_qg, 3)
+    f_kv = scatter5(KV, r_kv, 4)
     f_down = scatter5(DOWN, r_down, 0)
     f_mlp = scatter5(MLP, r_mlp, 1)
-    f_kv = scatter5(KV, r_kv, 4)
     f_out = scatter5(OUT, r_out, 2)
     f_qg = finish(f_qg, CQ, CG)
+    f_kv = finish(f_kv, CK, CV, VTILE)
     f_down = finish(f_down, CMD)
     f_mlp = finish(f_mlp, CMG, CMU)
-    f_kv = finish(f_kv, CK, CV, VTILE)
     f_out = finish(f_out, CO)
     c_sent()
-    put_out.wait()
-    put_gin.wait()
     most = pl.ds(CQ, TOTAL - CQ)
     sent = (
         W.at[0, 0, 0:3], W.at[0, 0:3, :, :, 0:CQ], W.at[0, 0:2, :, :, most], W.at[0, 0, :, :, most], W.at[0:2], W.at[0],
@@ -1020,26 +1005,16 @@
     for copy in (e_first, e_rest, e_x, e_g, e_sec, e_norm):
         copy.wait_send()
     remote(FSEND, FRECV, ex_s.at[7], ex_r.at[9], sibling).wait_send()
-    for ref, at in ((OUT8, 8), (OUTVEC, 9), (OUTW, 10)):
-        pltpu.make_async_copy(ref, ref, loc.at[at]).wait()
 
 
 def hand_over(*refs):
-    vec, results, smalls, outs, rows, held = refs[0], refs[1:11], refs[11:15], refs[15:25], refs[25], refs[26:36]
-    sems = refs[36]
-    fetch = [pltpu.make_async_copy(a, b, sems.at[i]) for i, (a, b) in enumerate(zip(results, held))]
-    write = [pltpu.make_async_copy(a, b, sems.at[10 + i]) for i, (a, b) in enumerate(zip(held, outs))]
-    last = pltpu.make_async_copy(vec, rows, sems.at[20])
-    for copy in fetch:
+    vec, results, smalls, outs, sems = refs[0], refs[1:11], refs[11:15], refs[15:25], refs[25]
+    copies = [pltpu.make_async_copy(a, b, sems.at[i]) for i, (a, b) in enumerate(zip(results, outs))]
+    for copy in copies:
         copy.start()
-    last.start()
-    for a, b in zip(fetch, write):
-        a.wait()
-        b.start()
-    last.wait()
     for i, ref in enumerate(smalls):
-        ref[...] = rows[i : i + 1, 0:8]
-    for copy in write:
+        ref[...] = vec[i : i + 1, 0:8]
+    for copy in copies:
         copy.wait()
 
 
@@ -1056,14 +1031,14 @@
     return [
         b(4, 4, 4, 16, TOTAL), b(4, 4, 4, 16, TOTAL), b(2, 2, 4, 16, TOTAL), b(2, 4, 4, 16, TOTAL),
         b(2, 2, 16, TOTAL), b(2, 4, 16, TOTAL), b(3, 4, 16, CQ), b(3, 16, TOTAL),
-        b(256, 1024), b(256, 1024), f(8, 1792), b(2, 8, 1024), b(6, 8, 1728), f(8, 128), f(2, 8, 1024), f(6, 8, 1728), f(8, 128),
-        b(2, 128, 1024), b(16, TOTAL), b(2, 16, TOTAL), f(8, 1024), f(8, 1024),
+        b(256, 1024), b(256, 1024), f(8, 1792), b(2, 8, 1024), b(6, 8, 1728), f(8, 128),
+        b(16, TOTAL), b(2, 16, TOTAL), f(8, 1024), f(8, 1024),
         f(256, 128), f(256, 128), f(4, 256, 128),
         b(256, 1024), b(1024, 256), b(1024, 256), b(256, 512), b(256, 512), b(256, 512), b(256, 512),
-        b(256, WIDE), b(256, WIDE), f(256, WIDE), b(2, 256, 256), f(2, 256, 256), f(256, WIDE), f(256, WIDE),
+        b(256, WIDE), b(256, WIDE), f(256, WIDE), b(2, 256, 256), f(256, WIDE), f(256, WIDE),
         b(REAL, 256), b(REAL, 256), b(3, REAL, 256), b(WIDE, 256), b(WIDE, 256),
         b(256, WIDE), f(256, 1024), b(256, 1024), b(256, 1024), b(128, 1024), b(128, 1024), f(128, 1024),
-        b(256, 1024), b(128, 1024), f(128, 1024),
+        b(256, 1024), b(128, 1024),
         b(256, 1024), f(256, WIDE), f(256, WIDE), b(256, WIDE), b(256, WIDE), b(256, WIDE),
         f(256, 1024), b(256, WIDE), b(256, 512), b(256, 512), b(256, WIDE),
         f(8, TOTAL), f(8, TOTAL), f(8, TOTAL),
@@ -1086,12 +1061,12 @@
     vectors = (ln1_gain, ln1_bias, ln2_gain, ln2_bias)
     out, gin, vec, *grads = pl.pallas_call(
         kernel,
-        out_shape=results[:2] + [jax.ShapeDtypeStruct((8, 128), F32)] + results[2:],
+        out_shape=[pltpu.VMEM(r.shape, r.dtype) for r in results[:2] + [jax.ShapeDtypeStruct((8, 128), F32)] + results[2:]],
         in_specs=[here] * 4 + [anywhere] * 12,
-        out_specs=[anywhere] * 11,
+        out_specs=[here] * 11,
         scratch_shapes=scratch(),
         compiler_params=pltpu.CompilerParams(
-            collective_id=0, has_side_effects=True, vmem_limit_bytes=64 << 20
+            collective_id=0, has_side_effects=True, vmem_limit_bytes=63 << 20
         ),
         name="block",
     )(
@@ -1101,12 +1076,10 @@
     *smalls, out, gin, gq, gk, gv, gg, go, gmg, gmu, gmd = pl.pallas_call(
         hand_over,
         out_shape=[small] * 4 + results,
-        in_specs=[anywhere] * 11,
+        in_specs=[here] * 11,
         out_specs=[here] * 4 + [anywhere] * 10,
-        scratch_shapes=[pltpu.VMEM((8, 128), F32)]
-        + [pltpu.VMEM(r.shape, r.dtype) for r in results]
-        + [pltpu.SemaphoreType.DMA((21,))],
-        compiler_params=pltpu.CompilerParams(vmem_limit_bytes=64 << 20),
+        scratch_shapes=[pltpu.SemaphoreType.DMA((10,))],
+        compiler_params=pltpu.CompilerParams(vmem_limit_bytes=32 << 20),
         name="hand_over",
     )(vec, out, gin, *grads)
     a, b, c, d = (v.reshape(8) for v in smalls)

time: 128 us -> 125 us (0.977)
  Pallas kernels: 127 us -> 124 us
    pallas_call x2, Pallas kernels: 127 us -> 124 us  [the longest x1 123 us: per_device(): pl.pallas_call(kernel, out_shape=[pltpu.VMEM(r.shape, r.dtype) for r in r...]
where the time goes in v3:
time: 125 us
  Pallas kernels  124 us (99%)
    pallas_call x1, Pallas kernels, per_device(): pl.pallas_call(kernel, out_shape=[pltpu.VMEM(r.shape, r.dtype) for r in r...  123 us

profile of v3, /device:TPU:1, one launch (start us, length us, event | category | flops | bytes accessed | tf_op | source)
XLA Modules:
  0.0 125.1 jit_solution(11044928532583011298)
XLA Ops:
  0.7 122.8 %block.1 = (bf16[128,1024]{1,0:T(8,128)(2,1)S(1)}, bf16[128,1024]{1,0:T(8,128)(2,1)S(1)}, f32[8,128]{1,0:T(8,128)S(1)}, f32[8,1024]{1,0:T(8,128)S(1)}, f32[8,102...) custom-call(bf16[1,8]{1,0:T(2,128)(2,1)} %bitcast.20, ...), custom_call_target="tpu_custom_call" | custom-call | tf_op jit(solution)/shard_map/block/pallas_call | solution.py:1062
  123.4 1.5 %hand_over.1 = (f32[1,8]{1,0:T(1,128)}, f32[1,8]{1,0:T(1,128)}, f32[1,8]{1,0:T(1,128)}, f32[1,8]{1,0:T(1,128)}, bf16[128,1024]{1,0:T(8,128)(2,1)}, /*index=5*/bf...) custom-call(f32[8,128]{1,0:T(8,128)S(1)} %get-tuple-element.39.refs_, ...), custom_call_target="tpu_custom_call" | custom-call | tf_op jit(solution)/shard_map/hand_over/pallas_call | solution.py:1076

commit v4 on v3

--- a/solution.py
+++ b/solution.py
@@ -286,7 +286,7 @@
         return W[:, :, :, :, col : col + n].reshape(1024, n)
 
     def wrows(i, col, n):
-        return W[i, :, :, :, col : col + n].reshape(256, n)
+        return W[2 * i : 2 * i + 2, :, :, :, col : col + n].reshape(512, n)
 
     def fwd(a, col, n, emit):
         for at in range(0, n, 256):
@@ -499,13 +499,13 @@
 
     def out_body(i):
         r = mm_nt(GATED[...], wrows(i, CO, WIDE))
-        s = pl.ds(i * 256, 256)
+        s = pl.ds(i * 512, 512)
         MID[:, s] = r
         SB[:, s] = r.astype(BF16)
         remote(SB.at[:, s], RB.at[:, s], ex_s.at[3], ex_r.at[3], sibling).start()
 
     def out():
-        each(4, out_body)
+        each(2, out_body)
 
     e_mid = remote(SB, RB, ex_s.at[3], ex_r.at[3], sibling)
 
@@ -710,14 +710,14 @@
 
     def second_body(i):
         r = mm_nt(GGL[...], wrows(i, CMG, WIDE)) + mm_nt(GUL[...], wrows(i, CMU, WIDE))
-        s = pl.ds(i * 256, 256)
+        s = pl.ds(i * 512, 512)
         GM[:, s] = r
         SB[:, s] = r.astype(BF16)
         remote(SB.at[:, s], RB2.at[:, s], ex_s.at[5], ex_r.at[5], sibling).start()
 
     def gs():
         e_mid.wait_send()
-        each(4, second_body)
+        each(2, second_body)
 
     e_sec = remote(SB, RB2, ex_s.at[5], ex_r.at[5], sibling)
 
@@ -825,23 +825,23 @@
 
     def down_body(i):
         r = mm_nt(HID[...], wrows(i, CMD, WIDE))
-        s = pl.ds(i * 256, 256)
+        s = pl.ds(i * 512, 512)
         OWN1[:, s] = r[0:128] * c0 + r[128:256] * c1
         SBO[:, s] = (r[0:128] * c1 + r[128:256] * c0).astype(BF16)
 
     e_out = remote(SBO, RBO, ex_s.at[4], ex_r.at[4], sibling)
     def down():
-        each(4, down_body)
+        each(2, down_body)
         e_out.start()
 
     def normed_first(i):
         r = mm_nt(GQ[...], wrows(i, CQ, 512)) + mm_nt(GGP[...], wrows(i, CG, WIDE))
-        MID[:, pl.ds(i * 256, 256)] = r
+        MID[:, pl.ds(i * 512, 512)] = r
 
     def pn1():
         e_out.wait_recv()
         out_ref[...] = (MID[rows_own, :] + OWN1[...] + RBO[...].astype(F32)).astype(BF16)
-        each(4, normed_first)
+        each(2, normed_first)
 
     def kvb():
         gvs = []
@@ -859,7 +859,7 @@
         grad(NORMT, GV, CV)
 
     def normed_body(i):
-        s = pl.ds(i * 256, 256)
+        s = pl.ds(i * 512, 512)
         r = MID[:, s] + mm_nt(GK[...], wrows(i, CK, 512)) + mm_nt(GV[...], wrows(i, CV, WIDE))
         OWN1[:, s] = r[0:128] * c0 + r[128:256] * c1
         SBO[:, s] = (r[0:128] * c1 + r[128:256] * c0).astype(BF16)
@@ -867,7 +867,7 @@
 
     def pn2():
         e_out.wait_send()
-        each(4, normed_body)
+        each(2, normed_body)
 
     e_norm = remote(SBO, RB3, ex_s.at[6], ex_r.at[6], sibling)
 

time: 125 us -> 125 us (level)
  no operation moved by 1% of the time
where the time goes in v4:
time: 125 us
  Pallas kernels  124 us (99%)
    pallas_call x1, Pallas kernels, per_device(): pl.pallas_call(kernel, out_shape=[pltpu.VMEM(r.shape, r.dtype) for r in r...  122 us

profile of v4, /device:TPU:1, one launch (start us, length us, event | category | flops | bytes accessed | tf_op | source)
XLA Modules:
  0.0 124.8 jit_solution(8886847697840446256)
XLA Ops:
  0.7 122.4 %block.1 = (bf16[128,1024]{1,0:T(8,128)(2,1)S(1)}, bf16[128,1024]{1,0:T(8,128)(2,1)S(1)}, f32[8,128]{1,0:T(8,128)S(1)}, f32[8,1024]{1,0:T(8,128)S(1)}, f32[8,102...) custom-call(bf16[1,8]{1,0:T(2,128)(2,1)} %bitcast.20, ...), custom_call_target="tpu_custom_call" | custom-call | tf_op jit(solution)/shard_map/block/pallas_call | solution.py:1062
  123.1 1.5 %hand_over.1 = (f32[1,8]{1,0:T(1,128)}, f32[1,8]{1,0:T(1,128)}, f32[1,8]{1,0:T(1,128)}, f32[1,8]{1,0:T(1,128)}, bf16[128,1024]{1,0:T(8,128)(2,1)}, /*index=5*/bf...) custom-call(f32[8,128]{1,0:T(8,128)S(1)} %get-tuple-element.39.refs_, ...), custom_call_target="tpu_custom_call" | custom-call | tf_op jit(solution)/shard_map/hand_over/pallas_call | solution.py:1076
